TPU v7x, 512 devices: a whole 4x8x8 slice. The times are simulated.
512 devices in a mesh: mode: 64 (over y, z), real: 8 (over x, core).
Axes of the slice: x: 4, y: 8, z: 8, core: 2. Of those that a mesh axis runs over, the one named last changes fastest.
Arguments:
- input_field: bfloat16 [2, 8, 256, 16384], P(None, 'real', 'mode'), may hold values from -6 to 6
- kerr_coeff: bfloat16 [64, 64, 64], P('mode'), may hold values from -0.1875 to 0.1875
- block_list: int32 [64, 4], P('mode'), may hold values from 0 to 31
Outputs:
- density: float32 [512, 2, 256, 256], P('mode', None, 'real')
All inputs are finite; a program needn't handle non-finite values.
Results may differ from a plain program's by a relative error of at most 0.0085.
Values may be sent and summed in bfloat16 or wider, within the bound.
No kernel may reach another device: no remote copies, remote signals or barrier semaphores. Data moves between devices by JAX's collectives and lax.ppermute only.
A program may use at most 64 MiB of HBM per device.

v0:
```python
import math

import jax
import jax.numpy as jnp
from jax import lax
from jax.sharding import Mesh
from jax.sharding import PartitionSpec as P

MB = 8
FT = 128
NT = 16384
FB = 32
MODE = ("mode_0", "mode_1")


kerr_strength = 0.25


def cut_along(array, dim, count):
    shape = array.shape
    parts = array.reshape(*shape[:dim], count, shape[dim] // count, *shape[dim + 1 :])
    return jnp.moveaxis(parts, dim, 0)


def in_order(parts, dim):
    parts = jnp.moveaxis(parts, 0, dim)
    shape = parts.shape
    return parts.reshape(*shape[:dim], shape[dim] * shape[dim + 1], *shape[dim + 2 :])


def moved_by_axis(parts, axes, order):
    inside = parts.shape[1:]
    filled = parts.reshape(*(lax.axis_size(a) for a in axes), *inside)
    for k in order:
        filled = lax.all_to_all(filled, axes[k], k, k, tiled=True)
    return filled.reshape(-1, *inside)


def stepwise_exchange(array, axes, order, split_dim, concat_dim):
    parts = cut_along(array, split_dim, lax.axis_size(axes))
    return in_order(moved_by_axis(parts, axes, order), concat_dim)


def from_everyone(array, axis):
    copies = jnp.broadcast_to(array, (lax.axis_size(axis), *array.shape))
    return lax.all_to_all(copies, axis, split_axis=0, concat_axis=0, tiled=True)


def gather_directly(array, axis, dim):
    parts = from_everyone(array, axis)
    return in_order(parts, dim)


def kerr_terms(field_blocks, coeff_group, block_group):
    mode_l = jnp.take(field_blocks, block_group[:, 1], axis=2).astype(jnp.float32)
    mode_m = jnp.take(field_blocks, block_group[:, 2], axis=2).astype(jnp.float32)
    mode_n = jnp.take(field_blocks, block_group[:, 3], axis=2).astype(jnp.float32)
    realiz = field_blocks.shape[1]
    group_size = block_group.shape[0]
    steps_local = field_blocks.shape[4]
    prod_re = (
        mode_m[0][:, :, :, None, :] * mode_n[0][:, :, None, :, :]
        + mode_m[1][:, :, :, None, :] * mode_n[1][:, :, None, :, :]
    )
    prod_im = (
        mode_m[1][:, :, :, None, :] * mode_n[0][:, :, None, :, :]
        - mode_m[0][:, :, :, None, :] * mode_n[1][:, :, None, :, :]
    )
    pairs = (
        jnp.stack([prod_re, prod_im])
        .reshape(2, realiz, group_size, MB * MB, steps_local)
        .astype(jnp.bfloat16)
    )
    weighted = jnp.einsum(
        "kab,crkbt->crkat", coeff_group, pairs, preferred_element_type=jnp.float32
    )
    weighted = weighted.reshape(2, realiz, group_size, MB, MB, steps_local)
    term_re = jnp.sum(
        weighted[0] * mode_l[0][:, :, None] - weighted[1] * mode_l[1][:, :, None], axis=3
    )
    term_im = jnp.sum(
        weighted[0] * mode_l[1][:, :, None] + weighted[1] * mode_l[0][:, :, None], axis=3
    )
    one_hot = (
        block_group[:, 0][:, None] == jnp.arange(field_blocks.shape[2], dtype=jnp.int32)[None, :]
    ).astype(jnp.float32)
    return jnp.einsum(
        "kg,crkpt->crgpt", one_hot, jnp.stack([term_re, term_im]), precision=lax.Precision.HIGHEST
    )


def phase_table(extent, modulus):
    index_a = jnp.arange(extent, dtype=jnp.int32)[:, None]
    index_b = jnp.arange(extent, dtype=jnp.int32)[None, :]
    angle = 2.0 * math.pi / modulus * (index_a * index_b % modulus).astype(jnp.float32)
    return (jnp.cos(angle), -jnp.sin(angle))


def first_pass(table, data):
    table_high = table.astype(jnp.bfloat16)
    table_low = (table - table_high.astype(jnp.float32)).astype(jnp.bfloat16)
    upper = jnp.einsum("kn,rmnj->rmkj", table_high, data, preferred_element_type=jnp.float32)
    return upper + jnp.einsum("kn,rmnj->rmkj", table_low, data, preferred_element_type=jnp.float32)


def second_pass(table, data):
    return jnp.einsum("jn,rmkn->rmjk", table, data, precision=lax.Precision.HIGH)


def transform(by_mode):
    realiz = by_mode.shape[1]
    local_modes = by_mode.shape[2]
    signal = by_mode.reshape(2, realiz, local_modes, FT, FT)
    four_re, four_im = phase_table(FT, FT)
    twist_re, twist_im = phase_table(FT, NT)
    half_re = first_pass(four_re, signal[0]) - first_pass(four_im, signal[1])
    half_im = first_pass(four_re, signal[1]) + first_pass(four_im, signal[0])
    turned_re = half_re * twist_re - half_im * twist_im
    turned_im = half_re * twist_im + half_im * twist_re
    out_re = (second_pass(four_re, turned_re) - second_pass(four_im, turned_im)) / FT
    out_im = (second_pass(four_re, turned_im) + second_pass(four_im, turned_re)) / FT
    return jnp.stack([out_re, out_im]).astype(jnp.bfloat16)


def gram_parts(rows_part, cols_part):
    quarters = jnp.einsum(
        "crpbf,drqbf->bcdpq", rows_part, cols_part, preferred_element_type=jnp.float32
    )
    return jnp.stack(
        [quarters[:, 0, 0] + quarters[:, 1, 1], quarters[:, 1, 0] - quarters[:, 0, 1]], axis=1
    )


def shards(input_field, kerr_coeff, block_list):
    timed = stepwise_exchange(input_field, MODE, (0, 1), 3, 2)
    realiz = timed.shape[1]
    width = timed.shape[2]
    steps_local = timed.shape[3]
    field_blocks = timed.reshape(2, realiz, width // MB, MB, steps_local)
    initial = jnp.zeros(field_blocks.shape, jnp.float32)
    running = initial
    coeff_piece = gather_directly(kerr_coeff, MODE, 0)
    block_piece = gather_directly(block_list, MODE, 0)
    block_count = block_piece.shape[0]
    coeff_groups = coeff_piece.reshape(
        block_count // 8, 8, coeff_piece.shape[1], coeff_piece.shape[2]
    )
    block_groups = block_piece.reshape(block_count // 8, 8, 4)

    def one_group(carried, groups):
        return (carried + kerr_terms(field_blocks, groups[0], groups[1]), None)

    running, unused = lax.scan(one_group, running, (coeff_groups, block_groups))
    kerr_sum = running
    kerr_sum = kerr_sum.reshape(2, realiz, width, steps_local)
    base = timed.astype(jnp.float32)
    stepped = jnp.stack(
        [base[0] - kerr_strength * kerr_sum[1], base[1] + kerr_strength * kerr_sum[0]]
    ).astype(jnp.bfloat16)
    by_mode = lax.all_to_all(stepped, MODE, split_axis=2, concat_axis=3, tiled=True)
    spectrum = transform(by_mode)
    banded = lax.all_to_all(spectrum, MODE, split_axis=3, concat_axis=2, tiled=True)
    bands_dev = banded.shape[3] * FT // FB
    spec_bands = banded.reshape(2, realiz, width, bands_dev, FB)
    scale = 1.0 / (FB * realiz * lax.axis_size("real"))
    row_count = width // lax.axis_size("real")
    row_first = lax.axis_index("real") * row_count
    shard_piece = gather_directly(spec_bands, "real", 1)
    own_part = lax.dynamic_slice_in_dim(shard_piece, row_first, row_count, 2)
    return gram_parts(own_part, shard_piece) * scale


def solution(mesh):
    finer = Mesh(mesh.devices.reshape(8, 8, mesh.shape["real"]), ("mode_0", "mode_1", "real"))
    return jax.shard_map(
        shards,
        mesh=finer,
        in_specs=(P(None, "real", MODE, None), P(MODE, None, None), P(MODE, None)),
        out_specs=P(MODE, None, "real", None),
        check_vma=False,
    )
```

profile of v0, /device:TPU:1, one launch (start us, length us, event | category | flops | bytes accessed | tf_op | source)
XLA Modules:
  0.0 193.4 jit_solution(13753208739281754765)
XLA Ops:
  0.0 1.1 reshape.514
  1.3 16.7 %all_to_all.55 = bf16[8,8,2,1,4,256]{5,4,1,2,3,0:T(4,128)(2,1)S(1)} all-to-all(bf16[8,8,2,1,4,256]{5,4,1,2,3,0:T(4,128)(2,1)S(1)} %copy.151), channel_id=1, replica_groups=mesh['mode_0'=8,'mode_1'=8,'real'=8] {'mode_0'}, dimensions={0} | all-to-all | bytes 524288 | tf_op jit(solution)/shard_map/all_to_all | solution.py:35
  18.1 1.3 broadcast_in_dim.19
  19.4 13.3 %all-to-all-start.2 = ((s32[64,1,4]{2,1,0:T(1,128)}), s32[64,1,4]{2,1,0:T(1,128)S(1)}, u32[]{:S(2)}, u32[]{:S(2)}) async-start(s32[64,1,4]{2,1,0:T(1,128)} %broadcast_in_dim.19), calls=%async_computation.2 | async-start | bytes 65536 | tf_op jit(solution)/shard_map/all_to_all | solution.py:46
  32.7 0.8 copy.152
  33.5 9.9 %all-to-all-done.2 = s32[64,1,4]{2,1,0:T(1,128)S(1)} async-done(((s32[64,1,4]{2,1,0:T(1,128)}), s32[64,1,4]{2,1,0:T(1,128)S(1)}, u32[]{:S(2)}, u32[]{:S(2)}) %all-to-all-start.2) | async-done | bytes 1056 | tf_op jit(solution)/shard_map/all_to_all | solution.py:46
  43.5 3.4 %all-to-all-start.1 = ((bf16[8,8,2,1,4,256]{5,4,0,2,3,1:T(4,128)(2,1)}), bf16[8,8,2,1,4,256]{5,4,0,2,3,1:T(4,128)(2,1)S(1)}, u32[]{:S(2)}, u32[]{:S(2)}) async-start(bf16[8,8,2,1,4,256]{5,4,0,2,3,1:T(4,128)(2,1)} %copy.152), calls=%async_computation.1 | async-start | bytes 524288 | tf_op jit(solution)/shard_map/all_to_all | solution.py:35
  47.2 1.5 reshape.580
  48.7 7.5 %all-to-all-done.1 = bf16[8,8,2,1,4,256]{5,4,0,2,3,1:T(4,128)(2,1)S(1)} async-done(((bf16[8,8,2,1,4,256]{5,4,0,2,3,1:T(4,128)(2,1)}), bf16[8,8,2,1,4,256]{5,4,0,2,3,1:T(4,128)(2,1)S(1)}, u32[]{:S(2)}, u32[]{:S(2)}) %all-to-all-start.1) | async-done | bytes 262176 | tf_op jit(solution)/shard_map/all_to_all | solution.py:35
  56.2 4.6 %all-to-all-start.3 = ((bf16[64,2,2048]{2,1,0:T(2,128)(2,1)}), bf16[64,2,2048]{2,1,0:T(2,128)(2,1)S(1)}, u32[]{:S(2)}, u32[]{:S(2)}) async-start(bf16[64,2,2048]{2,1,0:T(2,128)(2,1)} %reshape.580), calls=%async_computation.3 | async-start | bytes 1048576 | tf_op jit(solution)/shard_map/all_to_all | solution.py:46
  62.1 13.4 %all-to-all-done.3 = bf16[64,2,2048]{2,1,0:T(2,128)(2,1)S(1)} async-done(((bf16[64,2,2048]{2,1,0:T(2,128)(2,1)}), bf16[64,2,2048]{2,1,0:T(2,128)(2,1)S(1)}, u32[]{:S(2)}, u32[]{:S(2)}) %all-to-all-start.3) | async-done | bytes 524320 | tf_op jit(solution)/shard_map/all_to_all | solution.py:46
  75.5 0.7 reshape.581
  76.1 27.8 %while.11 = (s32[]{:T(128)}, f32[2,1,32,8,256]{4,2,3,0,1:T(8,128)S(1)}, s32[8,8,4]{1,2,0:T(4,128)S(1)}, bf16[2,1,32,8,256]{4,3,2,1,0:T(8,128)(2,1)S(1)}, bf16[8,...) while((s32[]{:T(128)}, f32[2,1,32,8,256]{4,2,3,0,1:T(8,128)S(1)}, ...), condition=%wide.region_3.5_spmd.clone, body=%wide.region_0.4_spmd.clone.sunk | while | flops 49745296 | bytes 7025519 | solution.py:153
  76.2 0.6 gather_fusion.1
  76.8 0.6 gather_fusion
  77.5 0.6 gather_fusion.2
  79.0 0.6 fusion.162
  79.7 0.6 gather_fusion.1
  80.2 0.6 gather_fusion
  80.9 0.6 gather_fusion.2
  82.5 0.6 fusion.162
  83.7 0.6 gather_fusion
  84.4 0.6 gather_fusion.2
  86.0 0.6 fusion.162
  86.6 0.6 gather_fusion.1
  87.2 0.6 gather_fusion
  89.4 0.6 fusion.162
  92.9 0.6 fusion.162
  96.4 0.6 fusion.162
  99.9 0.6 fusion.162
  103.3 0.6 fusion.162
  104.3 0.7 fusion.46
  105.0 0.9 pad_maximum_fusion
  105.9 1.1 copy.164
  107.0 6.9 %all-to-all-start.4 = ((bf16[2,1,256,256]{3,0,1,2:T(2,128)(2,1)}), bf16[2,1,256,256]{3,0,1,2:T(2,128)(2,1)S(1)}, u32[]{:S(2)}, u32[]{:S(2)}) async-start(bf16[2,1,256,256]{3,0,1,2:T(2,128)(2,1)} %copy.164), calls=%async_computation.4 | async-start | bytes 524288 | tf_op jit(solution)/shard_map/all_to_all | solution.py:160
  114.6 11.6 %all-to-all-done.4 = bf16[2,1,256,256]{3,0,1,2:T(2,128)(2,1)S(1)} async-done(((bf16[2,1,256,256]{3,0,1,2:T(2,128)(2,1)}), bf16[2,1,256,256]{3,0,1,2:T(2,128)(2,1)S(1)}, u32[]{:S(2)}, u32[]{:S(2)}) %all-to-all-start.4) | async-done | bytes 262176 | tf_op jit(solution)/shard_map/all_to_all | solution.py:160
  130.2 0.6 fusion.44
  130.8 0.6 fusion.40
  131.4 0.6 fusion.33
  132.0 0.6 fusion.32
  132.8 16.4 %all_to_all.56 = bf16[2,1,4,128,128]{4,2,1,0,3:T(4,128)(2,1)S(1)} all-to-all(bf16[2,1,4,128,128]{4,2,1,0,3:T(4,128)(2,1)S(1)} %copy.181), channel_id=1, replica_groups=mesh['mode_0'=8,'mode_1'=8,'real'=8] {'mode_0','mode_1'}, dimensions={3} | all-to-all | bytes 524288 | tf_op jit(solution)/shard_map/all_to_all | solution.py:162
  149.8 0.6 copy.184
  150.4 1.6 broadcast_in_dim.33
  152.0 10.6 %all-to-all-start.6 = ((bf16[8,2,1,256,8,32]{3,5,4,2,1,0:T(8,128)(2,1)}), bf16[8,2,1,256,8,32]{3,5,4,2,1,0:T(8,128)(2,1)S(1)}, u32[]{:S(2)}, u32[]{:S(2)}) async-start(bf16[8,2,1,256,8,32]{3,5,4,2,1,0:T(8,128)(2,1)} %broadcast_in_dim.33), calls=%async_computation.6 | async-start | bytes 4194304 | tf_op jit(solution)/shard_map/all_to_all | solution.py:46
  162.7 26.3 %all-to-all-done.6 = bf16[8,2,1,256,8,32]{3,5,4,2,1,0:T(8,128)(2,1)S(1)} async-done(((bf16[8,2,1,256,8,32]{3,5,4,2,1,0:T(8,128)(2,1)}), bf16[8,2,1,256,8,32]{3,5,4,2,1,0:T(8,128)(2,1)S(1)}, u32[]{:S(2)}, u32[]{:S(2)}) %all-to-all-start.6) | async-done | bytes 2097184 | tf_op jit(solution)/shard_map/all_to_all | solution.py:46
  189.4 1.3 copy.210
  190.7 1.7 fusion.21
  192.5 0.8 copy.189
  (182 shorter events, 24.3 us)
Async XLA Ops:
  0.0 46.9 %copy-start = (bf16[1,64,64]{2,1,0:T(8,128)(2,1)S(1)}, bf16[1,64,64]{2,1,0:T(8,128)(2,1)}, u32[]{:S(2)}) copy-start(bf16[1,64,64]{2,1,0:T(8,128)(2,1)} %param.8) | copy-start | bytes 24580
  19.4 24.1 %all-to-all-start.2 = ((s32[64,1,4]{2,1,0:T(1,128)}), s32[64,1,4]{2,1,0:T(1,128)S(1)}, u32[]{:S(2)}, u32[]{:S(2)}) async-start(s32[64,1,4]{2,1,0:T(1,128)} %broadcast_in_dim.19), calls=%async_computation.2 | async-start | bytes 65536 | tf_op jit(solution)/shard_map/all_to_all | solution.py:46
  43.5 12.7 %all-to-all-start.1 = ((bf16[8,8,2,1,4,256]{5,4,0,2,3,1:T(4,128)(2,1)}), bf16[8,8,2,1,4,256]{5,4,0,2,3,1:T(4,128)(2,1)S(1)}, u32[]{:S(2)}, u32[]{:S(2)}) async-start(bf16[8,8,2,1,4,256]{5,4,0,2,3,1:T(4,128)(2,1)} %copy.152), calls=%async_computation.1 | async-start | bytes 524288 | tf_op jit(solution)/shard_map/all_to_all | solution.py:35
  56.2 19.2 %all-to-all-start.3 = ((bf16[64,2,2048]{2,1,0:T(2,128)(2,1)}), bf16[64,2,2048]{2,1,0:T(2,128)(2,1)S(1)}, u32[]{:S(2)}, u32[]{:S(2)}) async-start(bf16[64,2,2048]{2,1,0:T(2,128)(2,1)} %reshape.580), calls=%async_computation.3 | async-start | bytes 1048576 | tf_op jit(solution)/shard_map/all_to_all | solution.py:46
  107.0 19.2 %all-to-all-start.4 = ((bf16[2,1,256,256]{3,0,1,2:T(2,128)(2,1)}), bf16[2,1,256,256]{3,0,1,2:T(2,128)(2,1)S(1)}, u32[]{:S(2)}, u32[]{:S(2)}) async-start(bf16[2,1,256,256]{3,0,1,2:T(2,128)(2,1)} %copy.164), calls=%async_computation.4 | async-start | bytes 524288 | tf_op jit(solution)/shard_map/all_to_all | solution.py:160
  152.0 37.0 %all-to-all-start.6 = ((bf16[8,2,1,256,8,32]{3,5,4,2,1,0:T(8,128)(2,1)}), bf16[8,2,1,256,8,32]{3,5,4,2,1,0:T(8,128)(2,1)S(1)}, u32[]{:S(2)}, u32[]{:S(2)}) async-start(bf16[8,2,1,256,8,32]{3,5,4,2,1,0:T(8,128)(2,1)} %broadcast_in_dim.33), calls=%async_computation.6 | async-start | bytes 4194304 | tf_op jit(solution)/shard_map/all_to_all | solution.py:46
where the time goes:
time: 194 us; the launch traced here: 193 us
  waiting for transfers between devices  68.7 us (35%)
  starting transfers between devices  38.9 us (20%)
  blocking collectives  33.1 us (17%)
  local copies, waits for them, and re-layouts  28.6 us (15%)
  matrix products  14.1 us (7%)
  other arithmetic  8.07 us (4%)
    all_to_all x3, waiting for transfers between devices, from_everyone(): return lax.all_to_all(copies, axis, split_axis=0, concat_axis=0, tiled=True)  49.6 us
    all_to_all x3, starting transfers between devices, from_everyone(): return lax.all_to_all(copies, axis, split_axis=0, concat_axis=0, tiled=True)  28.6 us
    all_to_all x1, blocking collectives, moved_by_axis(): filled = lax.all_to_all(filled, axes[k], k, k, tiled=True)  16.7 us
    all_to_all x1, blocking collectives, shards(): lax.all_to_all(spectrum, MODE, split_axis=3, concat_axis=2, tiled=True)  16.4 us
    all_to_all x1, waiting for transfers between devices, shards(): lax.all_to_all(stepped, MODE, split_axis=2, concat_axis=3, tiled=True)  11.6 us
    all_to_all x1, waiting for transfers between devices, moved_by_axis(): filled = lax.all_to_all(filled, axes[k], k, k, tiled=True)  7.5 us
    all_to_all x1, starting transfers between devices, shards(): lax.all_to_all(stepped, MODE, split_axis=2, concat_axis=3, tiled=True)  6.89 us
    dot_general x8, matrix products, kerr_terms(): jnp.einsum('kg,crkpt->crgpt', one_hot, jnp.stack([term_re, term_im]), pre...  4.53 us
  transfers between devices with their start and end apart: 5, of which 5 were waited for; matrix products, arithmetic and copies ran while one was open for 2% of the time, Pallas kernels for 0%

commit v1 on v0

v1 whole, which is shorter than its diff:
```python
import math

import jax
import jax.numpy as jnp
import numpy as np
from jax import lax
from jax.experimental import pallas as pl
from jax.experimental.pallas import tpu as pltpu
from jax.sharding import Mesh
from jax.sharding import PartitionSpec as P

MB = 8
FT = 128
FB = 32
NMB = 32
NBLK = 64
MODES = 256
NDEV = 64
MODE = ("y", "z")
F32 = jnp.float32
BF16 = jnp.bfloat16

kerr_strength = 0.25

VMEM_LIMIT = 48 * 2**20


def params():
    return pltpu.CompilerParams(vmem_limit_bytes=VMEM_LIMIT)


def in_vmem():
    return pl.BlockSpec(memory_space=pltpu.VMEM)


def in_smem():
    return pl.BlockSpec(memory_space=pltpu.SMEM)


def pack_kernel(core_ref, list_ref, field_ref, coeff_ref, out_ref):
    core = core_ref[0]
    row = lax.broadcasted_iota(jnp.int32, (32, 64), 0) + 32 * core
    col = lax.broadcasted_iota(jnp.int32, (32, 64), 1)
    pick = (col == (row % MB) * MB + row // MB).astype(F32).astype(BF16)
    own = jnp.dot(pick, coeff_ref[0], preferred_element_type=F32)
    own = jnp.concatenate([own[:16], own[16:]], axis=1).astype(BF16)
    lane = lax.broadcasted_iota(jnp.int32, (8, 128), 1)
    index = jnp.zeros((8, 128), jnp.int32)
    for j in range(4):
        index = jnp.where(lane == j, list_ref[0, j], index)
    index = index.astype(F32).astype(BF16)
    for i in range(NDEV):
        pieces = []
        for tt in range(2):
            for part in range(2):
                pieces.append(
                    field_ref[part, 0, :, pl.ds((2 * i + tt) * 128, 128)].astype(F32)
                )
        out_ref[i, 0:16, :] = jnp.concatenate(pieces, axis=0).astype(BF16)
        out_ref[i, 16:32, :] = own
        out_ref[i, 32:40, :] = index


def pack(core, block_list, field, coeff):
    return pl.pallas_call(
        pack_kernel,
        out_shape=jax.ShapeDtypeStruct((NDEV, 40, 128), BF16),
        in_specs=[in_smem(), in_smem(), in_vmem(), in_vmem()],
        out_specs=in_vmem(),
        compiler_params=params(),
        name="pack",
    )(core, block_list, field, coeff)


def kerr_kernel(list_ref, data_ref, coeff_ref, out_ref, field, total):
    for b in range(NMB):
        first = data_ref[2 * b, 0:16, :].astype(F32)
        second = data_ref[2 * b + 1, 0:16, :].astype(F32)
        for tt in range(2):
            for part in range(2):
                at = 8 * tt + 4 * part
                field[part, b, :, tt * 128 : tt * 128 + 128] = jnp.concatenate(
                    [first[at : at + 4], second[at : at + 4]], axis=0
                )
    total[...] = jnp.zeros(total.shape, F32)

    def one_block(k, carry):
        at_p = list_ref[k, 0]
        at_l = list_ref[k, 1]
        at_m = list_ref[k, 2]
        at_n = list_ref[k, 3]
        n_re = field[0, at_n]
        n_im = field[1, at_n]
        pair_re = []
        pair_im = []
        for m in range(MB):
            m_re = field[0, at_m, m : m + 1, :]
            m_im = field[1, at_m, m : m + 1, :]
            pair_re.append(m_re * n_re + m_im * n_im)
            pair_im.append(m_im * n_re - m_re * n_im)
        pairs = jnp.concatenate(
            [jnp.concatenate(pair_re, axis=0), jnp.concatenate(pair_im, axis=0)], axis=1
        ).astype(BF16)
        low = coeff_ref[0, k]
        high = coeff_ref[1, k]
        table = jnp.concatenate(
            [low[:, :64], low[:, 64:], high[:, :64], high[:, 64:]], axis=0
        )
        weighted = jnp.dot(table, pairs, preferred_element_type=F32)
        term_re = jnp.zeros((MB, 256), F32)
        term_im = jnp.zeros((MB, 256), F32)
        for l in range(MB):
            w_re = weighted[8 * l : 8 * l + 8, :256]
            w_im = weighted[8 * l : 8 * l + 8, 256:]
            l_re = field[0, at_l, l : l + 1, :]
            l_im = field[1, at_l, l : l + 1, :]
            term_re = term_re + (w_re * l_re - w_im * l_im)
            term_im = term_im + (w_re * l_im + w_im * l_re)
        total[0, at_p] += term_re
        total[1, at_p] += term_im
        return carry

    lax.fori_loop(0, NBLK, one_block, 0, unroll=2)

    for b in range(NMB):
        new_re = field[0, b] - kerr_strength * total[1, b]
        new_im = field[1, b] + kerr_strength * total[0, b]
        new = (new_re, new_im)
        for half in range(2):
            pieces = []
            for tt in range(2):
                for part in range(2):
                    pieces.append(
                        new[part][4 * half : 4 * half + 4, tt * 128 : tt * 128 + 128]
                    )
            out_ref[2 * b + half] = jnp.concatenate(pieces, axis=0).astype(BF16)


def kerr_step(block_list, data, coeff):
    return pl.pallas_call(
        kerr_kernel,
        out_shape=jax.ShapeDtypeStruct((NDEV, 16, 128), BF16),
        in_specs=[in_smem(), in_vmem(), in_vmem()],
        out_specs=in_vmem(),
        scratch_shapes=[
            pltpu.VMEM((2, NMB, MB, 256), F32),
            pltpu.VMEM((2, NMB, MB, 256), F32),
        ],
        compiler_params=params(),
        name="kerr",
    )(block_list, data, coeff)


def dft_tables():
    a = np.arange(FT)
    angle = 2.0 * math.pi / FT * ((a[:, None] * a[None, :]) % FT)
    cos, sin = np.cos(angle), -np.sin(angle)
    first = np.block([[cos, -sin], [sin, cos]])
    small = 2.0 * math.pi / (FT * FT) * (a[:, None] * a[None, :])
    twist = np.stack([np.cos(small), -np.sin(small)])
    return (
        jnp.asarray(first, BF16),
        jnp.asarray(first / FT, BF16),
        jnp.asarray(twist, F32),
    )


def dft_kernel(first_ref, second_ref, twist_ref, data_ref, out_ref, rows):
    rows[...] = data_ref[...].astype(F32).reshape(1024, 128)
    columns = []
    for m in range(4):
        columns.append(
            jnp.concatenate(
                [rows[pl.ds(m, 128, stride=8), :], rows[pl.ds(4 + m, 128, stride=8), :]],
                axis=0,
            ).astype(BF16)
        )
    half = jnp.dot(
        first_ref[...], jnp.concatenate(columns, axis=1), preferred_element_type=F32
    )
    t_re = twist_ref[0]
    t_im = twist_ref[1]
    turned = []
    for m in range(4):
        h_re = half[:128, 128 * m : 128 * m + 128]
        h_im = half[128:, 128 * m : 128 * m + 128]
        turned.append(
            jnp.concatenate(
                [h_re * t_re - h_im * t_im, h_re * t_im + h_im * t_re], axis=1
            ).astype(BF16)
        )
    spectrum = lax.dot_general(
        second_ref[...],
        jnp.concatenate(turned, axis=0),
        (((1,), (1,)), ((), ())),
        preferred_element_type=F32,
    )
    for part in range(2):
        for m in range(4):
            rows[pl.ds(4 * part + m, 128, stride=8), :] = spectrum[
                128 * part : 128 * part + 128, 128 * m : 128 * m + 128
            ]
    out_ref[...] = rows[...].reshape(NDEV, 16, 128).astype(BF16)


def transform(data):
    first, second, twist = dft_tables()
    return pl.pallas_call(
        dft_kernel,
        out_shape=jax.ShapeDtypeStruct((NDEV, 16, 128), BF16),
        in_specs=[in_vmem()] * 4,
        out_specs=in_vmem(),
        scratch_shapes=[pltpu.VMEM((1024, 128), F32)],
        compiler_params=params(),
        name="dft",
    )(first, second, twist, data)


def order_kernel(data_ref, out_ref):
    for b in range(MODES // 16):
        group = [data_ref[4 * b + s].astype(F32) for s in range(4)]
        for h in range(2):
            for part in range(2):
                at = 8 * h + 4 * part
                piece = jnp.concatenate([g[at : at + 4] for g in group], axis=0).astype(BF16)
                for copy in range(4):
                    out_ref[copy, h, part, 16 * b : 16 * b + 16, :] = piece


def order(data):
    return pl.pallas_call(
        order_kernel,
        out_shape=jax.ShapeDtypeStruct((4, 2, 2, MODES, 128), BF16),
        in_specs=[in_vmem()],
        out_specs=in_vmem(),
        compiler_params=params(),
        name="order",
    )(data)


def gram_kernel(first_ref, own_ref, other_ref, out_ref):
    start = pl.multiple_of(first_ref[0], 32)
    lane = lax.broadcasted_iota(jnp.int32, (32, 128), 1) // FB
    for h in range(2):
        lefts = [[] for _ in range(8)]
        rights = []
        for data_ref in (own_ref, other_ref):
            for x in range(4):
                re = data_ref[x, h, 0]
                im = data_ref[x, h, 1]
                rights += [re, im]
                own_re = data_ref[x, h, 0, pl.ds(start, 32), :].astype(F32)
                own_im = data_ref[x, h, 1, pl.ds(start, 32), :].astype(F32)
                for band in range(4):
                    b_re = jnp.where(lane == band, own_re, 0.0)
                    b_im = jnp.where(lane == band, own_im, 0.0)
                    lefts[2 * band] += [b_re.astype(BF16), b_im.astype(BF16)]
                    lefts[2 * band + 1] += [b_im.astype(BF16), (-b_re).astype(BF16)]
        left = jnp.concatenate([jnp.concatenate(p, axis=1) for p in lefts], axis=0)
        right = jnp.concatenate(rights, axis=1)
        result = lax.dot_general(
            left, right, (((1,), (1,)), ((), ())), preferred_element_type=F32
        ) * (1.0 / 256.0)
        for band in range(4):
            for d in range(2):
                at = 64 * band + 32 * d
                out_ref[4 * h + band, d] = result[at : at + 32]


def gram(first_row, own, other):
    return pl.pallas_call(
        gram_kernel,
        out_shape=jax.ShapeDtypeStruct((8, 2, 32, MODES), F32),
        in_specs=[in_smem(), in_vmem(), in_vmem()],
        out_specs=in_vmem(),
        compiler_params=params(),
        name="gram",
    )(first_row, own, other)


def swap(array, axes):
    return lax.all_to_all(array, axes, split_axis=0, concat_axis=0, tiled=True)


def shards(input_field, kerr_coeff, block_list):
    core = lax.axis_index("c")
    chip = lax.axis_index("x")
    packed = pack(core.reshape(1), block_list, input_field, kerr_coeff)
    timed = swap(packed, MODE)
    coeff = lax.all_gather(timed[:, 16:32, :], "c", axis=0, tiled=False)
    indices = timed[:, 32, 0:4].astype(jnp.int32)
    stepped = kerr_step(indices, timed, coeff)
    spectrum = transform(swap(stepped, MODE))
    banded = order(swap(spectrum, MODE))
    own = swap(banded, ("x",))
    other = lax.ppermute(own, "c", ((0, 1), (1, 0)))
    first_row = (2 * chip + core) * 32
    return gram(first_row.reshape(1), own, other)


def solution(mesh):
    finer = Mesh(mesh.devices.reshape(8, 8, 4, 2), ("y", "z", "x", "c"))
    return jax.shard_map(
        shards,
        mesh=finer,
        in_specs=(P(None, ("x", "c"), MODE, None), P(MODE, None, None), P(MODE, None)),
        out_specs=P(MODE, None, ("x", "c"), None),
        check_vma=False,
    )
```

time: 194 us -> 116 us (0.60)
  waiting for transfers between devices: 68.7 us -> 2.26 us
  blocking collectives: 33.1 us -> 92.8 us
  starting transfers between devices: 38.9 us -> 6.64 us
  local copies, waits for them, and re-layouts: 28.6 us -> 2.36 us
  matrix products: 14.1 us -> 0 us
  Pallas kernels: 0 us -> 11.5 us
  other arithmetic: 8.07 us -> 0.03 us
    all_to_all x5 -> x0, waiting for transfers between devices: 68.7 us -> none  [the longest x3 49.6 us: from_everyone(): return lax.all_to_all(copies, axis, split_axis=0, concat_axis=0, tiled=True)]
    all_to_all x2 -> x4, blocking collectives: 33.1 us -> 87.3 us  [swap(): return lax.all_to_all(array, axes, split_axis=0, concat_axis=0, tiled=True)]
    all_to_all x5 -> x0, starting transfers between devices: 38.9 us -> none  [the longest x3 28.6 us: from_everyone(): return lax.all_to_all(copies, axis, split_axis=0, concat_axis=0, tiled=True)]
    dot_general x29 -> x0, matrix products: 14.1 us -> none  [the longest x8 4.53 us: kerr_terms(): jnp.einsum('kg,crkpt->crgpt', one_hot, jnp.stack([term_re, term_im]), pre...]
    gather x24 -> x0, local copies, waits for them, and re-layouts: 13.3 us -> none  [the longest x8 4.44 us: kerr_terms(): jnp.take(field_blocks, block_group[:, 1], axis=2).astype(jnp.float32)]
    pallas_call x0 -> x5, Pallas kernels: none -> 11.5 us  [the longest x1 8.5 us: kerr_step(): pl.pallas_call(kerr_kernel, out_shape=jax.ShapeDtypeStruct((NDEV, 16, 128...]
    ppermute x0 -> x1, starting transfers between devices: none -> 6.64 us  [shards(): other = lax.ppermute(own, 'c', ((0, 1), (1, 0)))]
    all_gather x0 -> x1, blocking collectives: none -> 5.52 us  [shards(): coeff = lax.all_gather(timed[:, 16:32, :], 'c', axis=0, tiled=False)]
  transfers between devices with their start and end apart: 5 -> 1, of which waited for: 5 -> 1; matrix products, arithmetic and copies ran while one was open for 2% -> 0% of each run, Pallas kernels for 0% -> 0%
where the time goes in v1:
time: 116 us
  blocking collectives  92.8 us (80%)
  Pallas kernels  11.5 us (10%)
  starting transfers between devices  6.64 us (6%)
  local copies, waits for them, and re-layouts  2.36 us (2%)
  waiting for transfers between devices  2.26 us (2%)
    all_to_all x4, blocking collectives, swap(): return lax.all_to_all(array, axes, split_axis=0, concat_axis=0, tiled=True)  87.3 us
    pallas_call x1, Pallas kernels, kerr_step(): pl.pallas_call(kerr_kernel, out_shape=jax.ShapeDtypeStruct((NDEV, 16, 128...  8.5 us
    ppermute x1, starting transfers between devices, shards(): other = lax.ppermute(own, 'c', ((0, 1), (1, 0)))  6.64 us
    all_gather x1, blocking collectives, shards(): coeff = lax.all_gather(timed[:, 16:32, :], 'c', axis=0, tiled=False)  5.52 us
    unnamed x12, local copies, waits for them, and re-layouts  2.34 us
  transfers between devices with their start and end apart: 1, of which 1 were waited for; matrix products, arithmetic and copies ran while one was open for 0% of the time, Pallas kernels for 0%

profile of v1, /device:TPU:1, one launch (start us, length us, event | category | flops | bytes accessed | tf_op | source)
XLA Modules:
  0.0 115.7 jit_solution(15235269894011313121)
XLA Ops:
  0.0 0.0 copy-start.5
  0.0 0.7 copy-done.5
  0.7 0.0 copy-start
  0.7 0.9 copy-done
  1.6 0.0 copy-start.4
  1.6 0.7 copy-done.4
  2.3 0.8 pack.1
  3.1 35.5 %all_to_all.20.data_ref = bf16[64,40,128]{2,1,0:T(8,128)(2,1)S(1)} all-to-all(bf16[64,40,128]{2,1,0:T(8,128)(2,1)S(1)} %pack.1), channel_id=1, replica_groups=mesh['y'=8,'z'=8,'x'=4,'c'=2] {'y','z'}, dimensions={0} | all-to-all | bytes 1310720 | tf_op jit(solution)/shard_map/all_to_all | solution.py:282
  38.6 5.5 %all-gather = bf16[128,16,128]{2,1,0:T(8,128)(2,1)S(1)} all-gather(bf16[64,16,128]{2,1,0:T(8,128)(2,1)S(1)} %slice.9), channel_id=2, replica_groups=mesh['y'=8,'z'=8,'x'=4,'c'=2] {'c'}, dimensions={0}, use_global_device_ids=true | all-gather | bytes 786432 | tf_op jit(solution)/shard_map/all_gather | solution.py:290
  44.1 8.5 %kerr.1 = bf16[64,16,128]{2,1,0:T(8,128)(2,1)S(1)} custom-call(s32[64,4]{1,0:T(8,128)S(1)} %bitcast.5, bf16[64,40,128]{2,1,0:T(8,128)(2,1)S(1)} %all_to_all.20.data_ref, bf16[2,64,16,128]{3,2,1,0:T(8,128)(2,1)S(1)} %bitcast.4), custom_call_target="tpu_custom_call" | custom-call | tf_op jit(solution)/shard_map/kerr/pallas_call | solution.py:140
  52.6 0.0 copy-start.1
  52.7 0.0 copy-start.2
  52.7 0.0 copy-start.3
  52.7 18.9 %all_to_all.21.data_ref = bf16[64,16,128]{2,1,0:T(8,128)(2,1)S(1)} all-to-all(bf16[64,16,128]{2,1,0:T(8,128)(2,1)S(1)} %kerr.1), channel_id=1, replica_groups=mesh['y'=8,'z'=8,'x'=4,'c'=2] {'y','z'}, dimensions={0} | all-to-all | bytes 524288 | tf_op jit(solution)/shard_map/all_to_all | solution.py:282
  71.5 0.0 copy-done.1
  71.6 0.0 copy-done.2
  71.6 0.0 copy-done.3
  71.6 0.6 dft.1
  72.2 17.8 %all_to_all.22.data_ref = bf16[64,16,128]{2,1,0:T(8,128)(2,1)S(1)} all-to-all(bf16[64,16,128]{2,1,0:T(8,128)(2,1)S(1)} %dft.1), channel_id=1, replica_groups=mesh['y'=8,'z'=8,'x'=4,'c'=2] {'y','z'}, dimensions={0} | all-to-all | bytes 524288 | tf_op jit(solution)/shard_map/all_to_all | solution.py:282
  90.0 0.1 order.1
  90.1 15.1 %all_to_all.23.own_ref = bf16[4,2,2,256,128]{4,3,2,1,0:T(8,128)(2,1)S(1)} all-to-all(bf16[4,2,2,256,128]{4,3,2,1,0:T(8,128)(2,1)S(1)} %order.1), channel_id=1, replica_groups=mesh['y'=8,'z'=8,'x'=4,'c'=2] {'x'}, dimensions={0} | all-to-all | bytes 2097152 | tf_op jit(solution)/shard_map/all_to_all | solution.py:282
  105.2 6.6 %collective-permute-start = (bf16[4,2,2,256,128]{4,3,2,1,0:T(8,128)(2,1)S(1)}, bf16[4,2,2,256,128]{4,3,2,1,0:T(8,128)(2,1)S(1)}, u32[]{:S(2)}, u32[]{:S(2)}) collective-permute-start(bf16[4,2,2,256,128]{4,3,2,1,0:T(8,128)(2,1)S(1)} %all_to_all.23.own_ref), channel_id=1, source_target_pairs={{0,1},{1,0},{2,3},{3,2},{4,5},{5,4},{6,7},{7,6},{8,9},{9,8},{10,11... | collective-permute-start | bytes 3145736 | tf_op jit(solution)/shard_map/ppermute | solution.py:296
  111.9 2.3 %collective-permute-done.other_ref = bf16[4,2,2,256,128]{4,3,2,1,0:T(8,128)(2,1)S(1)} collective-permute-done((bf16[4,2,2,256,128]{4,3,2,1,0:T(8,128)(2,1)S(1)}, bf16[4,2,2,256,128]{4,3,2,1,0:T(8,128)(2,1)S(1)}, u32[]{:S(2)}, u32[]{:S(2)}) %collective-permute-start) | collective-permute-done | bytes 1048608 | tf_op jit(solution)/shard_map/ppermute | solution.py:296
  114.1 1.5 %gram.1 = f32[8,2,32,256]{3,2,1,0:T(8,128)} custom-call(s32[1]{0:T(128)} %bitcast.first_ref, bf16[4,2,2,256,128]{4,3,2,1,0:T(8,128)(2,1)S(1)} %all_to_all.23.own_ref, bf16[4,2,2,256,128]{4,3,2,1,0:T(8,128)(2,1)S(1)} %collective-permute-done.other_ref), custom_call_target="tpu_custom_call" | custom-call | tf_op jit(solution)/shard_map/gram/pallas_call | solution.py:271
  (2 shorter events, 0.0 us)
Async XLA Ops:
  0.0 0.7 copy-start.5
  0.7 0.9 copy-start
  1.6 0.7 copy-start.4
  52.6 18.9 %copy-start.1 = (f32[2,128,128]{2,1,0:T(8,128)S(1)}, f32[2,128,128]{2,1,0:T(8,128)}, u32[]{:S(2)}) copy-start(f32[2,128,128]{2,1,0:T(8,128)} %constant.20.clone.twist_ref) | copy-start | bytes 393220
  52.7 18.9 %copy-start.2 = (bf16[256,256]{1,0:T(8,128)(2,1)S(1)}, bf16[256,256]{1,0:T(8,128)(2,1)}, u32[]{:S(2)}) copy-start(bf16[256,256]{1,0:T(8,128)(2,1)} %constant.19.clone.second_ref) | copy-start | bytes 393220
  52.7 18.9 %copy-start.3 = (bf16[256,256]{1,0:T(8,128)(2,1)S(1)}, bf16[256,256]{1,0:T(8,128)(2,1)}, u32[]{:S(2)}) copy-start(bf16[256,256]{1,0:T(8,128)(2,1)} %constant.18.clone.first_ref) | copy-start | bytes 393220
  105.2 8.9 %collective-permute-start = (bf16[4,2,2,256,128]{4,3,2,1,0:T(8,128)(2,1)S(1)}, bf16[4,2,2,256,128]{4,3,2,1,0:T(8,128)(2,1)S(1)}, u32[]{:S(2)}, u32[]{:S(2)}) collective-permute-start(bf16[4,2,2,256,128]{4,3,2,1,0:T(8,128)(2,1)S(1)} %all_to_all.23.own_ref), channel_id=1, source_target_pairs={{0,1},{1,0},{2,3},{3,2},{4,5},{5,4},{6,7},{7,6},{8,9},{9,8},{10,11... | collective-permute-start | bytes 3145736 | tf_op jit(solution)/shard_map/ppermute | solution.py:296

commit v2 on v1

--- a/solution.py
+++ b/solution.py
@@ -25,70 +25,93 @@
 VMEM_LIMIT = 48 * 2**20
 
 
-def params():
-    return pltpu.CompilerParams(vmem_limit_bytes=VMEM_LIMIT)
+def params(limit=VMEM_LIMIT):
+    return pltpu.CompilerParams(vmem_limit_bytes=limit)
 
 
 def in_vmem():
     return pl.BlockSpec(memory_space=pltpu.VMEM)
 
 
+def in_hbm():
+    return pl.BlockSpec(memory_space=pltpu.HBM)
+
+
 def in_smem():
     return pl.BlockSpec(memory_space=pltpu.SMEM)
 
 
-def pack_kernel(core_ref, list_ref, field_ref, coeff_ref, out_ref):
-    core = core_ref[0]
+def pack_kernel(place_ref, list_ref, field_hbm, coeff_hbm, out_ref, field, coeff, sems):
+    field_copy = pltpu.make_async_copy(field_hbm, field, sems.at[0])
+    coeff_copy = pltpu.make_async_copy(coeff_hbm, coeff, sems.at[1])
+    field_copy.start()
+    coeff_copy.start()
+    core = place_ref[0]
     row = lax.broadcasted_iota(jnp.int32, (32, 64), 0) + 32 * core
     col = lax.broadcasted_iota(jnp.int32, (32, 64), 1)
     pick = (col == (row % MB) * MB + row // MB).astype(F32).astype(BF16)
-    own = jnp.dot(pick, coeff_ref[0], preferred_element_type=F32)
+    lane = lax.broadcasted_iota(jnp.int32, (4, 128), 1)
+    line = lax.broadcasted_iota(jnp.int32, (4, 128), 0)
+    index = jnp.zeros((4, 128), jnp.int32)
+    for j in range(4):
+        index = jnp.where((lane == place_ref[1]) & (line == j), list_ref[0, j], index)
+    index = index.astype(F32).astype(BF16)
+    coeff_copy.wait()
+    own = jnp.dot(pick, coeff[0], preferred_element_type=F32)
     own = jnp.concatenate([own[:16], own[16:]], axis=1).astype(BF16)
-    lane = lax.broadcasted_iota(jnp.int32, (8, 128), 1)
-    index = jnp.zeros((8, 128), jnp.int32)
-    for j in range(4):
-        index = jnp.where(lane == j, list_ref[0, j], index)
-    index = index.astype(F32).astype(BF16)
     for i in range(NDEV):
-        pieces = []
+        for q in range(4):
+            out_ref[i, 4 + q] = own[4 * q : 4 * q + 4]
+        out_ref[i, 8] = index
+    field_copy.wait()
+    for i in range(NDEV):
         for tt in range(2):
             for part in range(2):
-                pieces.append(
-                    field_ref[part, 0, :, pl.ds((2 * i + tt) * 128, 128)].astype(F32)
-                )
-        out_ref[i, 0:16, :] = jnp.concatenate(pieces, axis=0).astype(BF16)
-        out_ref[i, 16:32, :] = own
-        out_ref[i, 32:40, :] = index
-
-
-def pack(core, block_list, field, coeff):
+                out_ref[i, 2 * tt + part] = field[
+                    part, 0, :, (2 * i + tt) * 128 : (2 * i + tt) * 128 + 128
+                ]
+
+
+def pack(place, block_list, field, coeff):
     return pl.pallas_call(
         pack_kernel,
-        out_shape=jax.ShapeDtypeStruct((NDEV, 40, 128), BF16),
-        in_specs=[in_smem(), in_smem(), in_vmem(), in_vmem()],
-        out_specs=in_vmem(),
-        compiler_params=params(),
+        out_shape=jax.ShapeDtypeStruct((NDEV, 9, 4, 128), BF16),
+        in_specs=[in_smem(), in_smem(), in_hbm(), in_hbm()],
+        out_specs=in_vmem(),
+        scratch_shapes=[
+            pltpu.VMEM(field.shape, BF16),
+            pltpu.VMEM(coeff.shape, BF16),
+            pltpu.SemaphoreType.DMA((2,)),
+        ],
+        compiler_params=params(60 * 2**20),
         name="pack",
-    )(core, block_list, field, coeff)
-
-
-def kerr_kernel(list_ref, data_ref, coeff_ref, out_ref, field, total):
+    )(place, block_list, field, coeff)
+
+
+def kerr_kernel(data_ref, coeff_ref, out_ref, field, total, listed, indices, sem):
+    index = jnp.sum(data_ref[:, 8].astype(F32), axis=0)
+    listed[...] = jnp.concatenate([index, index], axis=0).astype(jnp.int32)
+    list_copy = pltpu.make_async_copy(listed, indices, sem)
+    list_copy.start()
     for b in range(NMB):
-        first = data_ref[2 * b, 0:16, :].astype(F32)
-        second = data_ref[2 * b + 1, 0:16, :].astype(F32)
         for tt in range(2):
             for part in range(2):
-                at = 8 * tt + 4 * part
-                field[part, b, :, tt * 128 : tt * 128 + 128] = jnp.concatenate(
-                    [first[at : at + 4], second[at : at + 4]], axis=0
+                both = jnp.concatenate(
+                    [
+                        data_ref[2 * b, 2 * tt + part].astype(F32),
+                        data_ref[2 * b + 1, 2 * tt + part].astype(F32),
+                    ],
+                    axis=0,
                 )
-    total[...] = jnp.zeros(total.shape, F32)
+                field[part, b, :, tt * 128 : tt * 128 + 128] = both
+                total[part, b, :, tt * 128 : tt * 128 + 128] = both
+    list_copy.wait()
 
     def one_block(k, carry):
-        at_p = list_ref[k, 0]
-        at_l = list_ref[k, 1]
-        at_m = list_ref[k, 2]
-        at_n = list_ref[k, 3]
+        at_p = indices[0, k]
+        at_l = indices[1, k]
+        at_m = indices[2, k]
+        at_n = indices[3, k]
         n_re = field[0, at_n]
         n_im = field[1, at_n]
         pair_re = []
@@ -116,16 +139,14 @@
             l_im = field[1, at_l, l : l + 1, :]
             term_re = term_re + (w_re * l_re - w_im * l_im)
             term_im = term_im + (w_re * l_im + w_im * l_re)
-        total[0, at_p] += term_re
-        total[1, at_p] += term_im
+        total[0, at_p] -= kerr_strength * term_im
+        total[1, at_p] += kerr_strength * term_re
         return carry
 
-    lax.fori_loop(0, NBLK, one_block, 0, unroll=2)
+    lax.fori_loop(0, NBLK, one_block, 0, unroll=16)
 
     for b in range(NMB):
-        new_re = field[0, b] - kerr_strength * total[1, b]
-        new_im = field[1, b] + kerr_strength * total[0, b]
-        new = (new_re, new_im)
+        new = (total[0, b], total[1, b])
         for half in range(2):
             pieces = []
             for tt in range(2):
@@ -136,19 +157,22 @@
             out_ref[2 * b + half] = jnp.concatenate(pieces, axis=0).astype(BF16)
 
 
-def kerr_step(block_list, data, coeff):
+def kerr_step(data, coeff):
     return pl.pallas_call(
         kerr_kernel,
         out_shape=jax.ShapeDtypeStruct((NDEV, 16, 128), BF16),
-        in_specs=[in_smem(), in_vmem(), in_vmem()],
+        in_specs=[in_vmem(), in_vmem()],
         out_specs=in_vmem(),
         scratch_shapes=[
             pltpu.VMEM((2, NMB, MB, 256), F32),
             pltpu.VMEM((2, NMB, MB, 256), F32),
+            pltpu.VMEM((8, 128), jnp.int32),
+            pltpu.SMEM((8, 128), jnp.int32),
+            pltpu.SemaphoreType.DMA,
         ],
         compiler_params=params(),
         name="kerr",
-    )(block_list, data, coeff)
+    )(data, coeff)
 
 
 def dft_tables():
@@ -238,24 +262,25 @@
     )(data)
 
 
-def gram_kernel(first_ref, own_ref, other_ref, out_ref):
-    start = pl.multiple_of(first_ref[0], 32)
+def gram_kernel(place_ref, data_ref, own_ref, send_ref):
+    core = place_ref[0]
+    keep = pl.multiple_of(64 * place_ref[2] + 32 * core, 32)
+    give = pl.multiple_of(64 * place_ref[2] + 32 * (1 - core), 32)
     lane = lax.broadcasted_iota(jnp.int32, (32, 128), 1) // FB
     for h in range(2):
-        lefts = [[] for _ in range(8)]
+        lefts = [[] for _ in range(16)]
         rights = []
-        for data_ref in (own_ref, other_ref):
-            for x in range(4):
-                re = data_ref[x, h, 0]
-                im = data_ref[x, h, 1]
-                rights += [re, im]
-                own_re = data_ref[x, h, 0, pl.ds(start, 32), :].astype(F32)
-                own_im = data_ref[x, h, 1, pl.ds(start, 32), :].astype(F32)
+        for x in range(4):
+            rights += [data_ref[x, h, 0], data_ref[x, h, 1]]
+            for side, start in enumerate((keep, give)):
+                row_re = data_ref[x, h, 0, pl.ds(start, 32), :].astype(F32)
+                row_im = data_ref[x, h, 1, pl.ds(start, 32), :].astype(F32)
                 for band in range(4):
-                    b_re = jnp.where(lane == band, own_re, 0.0)
-                    b_im = jnp.where(lane == band, own_im, 0.0)
-                    lefts[2 * band] += [b_re.astype(BF16), b_im.astype(BF16)]
-                    lefts[2 * band + 1] += [b_im.astype(BF16), (-b_re).astype(BF16)]
+                    b_re = jnp.where(lane == band, row_re, 0.0)
+                    b_im = jnp.where(lane == band, row_im, 0.0)
+                    at = 8 * side + 2 * band
+                    lefts[at] += [b_re.astype(BF16), b_im.astype(BF16)]
+                    lefts[at + 1] += [b_im.astype(BF16), (-b_re).astype(BF16)]
         left = jnp.concatenate([jnp.concatenate(p, axis=1) for p in lefts], axis=0)
         right = jnp.concatenate(rights, axis=1)
         result = lax.dot_general(
@@ -264,18 +289,37 @@
         for band in range(4):
             for d in range(2):
                 at = 64 * band + 32 * d
-                out_ref[4 * h + band, d] = result[at : at + 32]
-
-
-def gram(first_row, own, other):
+                own_ref[4 * h + band, d] = result[at : at + 32]
+                send_ref[4 * h + band, d] = result[256 + at : 256 + at + 32].astype(BF16)
+
+
+def gram(place, data):
     return pl.pallas_call(
         gram_kernel,
+        out_shape=(
+            jax.ShapeDtypeStruct((8, 2, 32, MODES), F32),
+            jax.ShapeDtypeStruct((8, 2, 32, MODES), BF16),
+        ),
+        in_specs=[in_smem(), in_vmem()],
+        out_specs=(in_vmem(), in_vmem()),
+        compiler_params=params(),
+        name="gram",
+    )(place, data)
+
+
+def add_kernel(place_ref, own_ref, sent_ref, out_ref):
+    out_ref[...] = own_ref[...] + sent_ref[1 - place_ref[0]].astype(F32)
+
+
+def add(place, own, sent):
+    return pl.pallas_call(
+        add_kernel,
         out_shape=jax.ShapeDtypeStruct((8, 2, 32, MODES), F32),
         in_specs=[in_smem(), in_vmem(), in_vmem()],
         out_specs=in_vmem(),
         compiler_params=params(),
-        name="gram",
-    )(first_row, own, other)
+        name="add",
+    )(place, own, sent)
 
 
 def swap(array, axes):
@@ -283,19 +327,15 @@
 
 
 def shards(input_field, kerr_coeff, block_list):
-    core = lax.axis_index("c")
-    chip = lax.axis_index("x")
-    packed = pack(core.reshape(1), block_list, input_field, kerr_coeff)
-    timed = swap(packed, MODE)
-    coeff = lax.all_gather(timed[:, 16:32, :], "c", axis=0, tiled=False)
-    indices = timed[:, 32, 0:4].astype(jnp.int32)
-    stepped = kerr_step(indices, timed, coeff)
+    place = jnp.stack([lax.axis_index("c"), lax.axis_index(MODE), lax.axis_index("x")])
+    timed = swap(pack(place, block_list, input_field, kerr_coeff), MODE)
+    halves = timed[:, 4:8].reshape(NDEV, 16, 128)
+    coeff = lax.all_gather(halves, "c", axis=0, tiled=False)
+    stepped = kerr_step(timed, coeff)
     spectrum = transform(swap(stepped, MODE))
     banded = order(swap(spectrum, MODE))
-    own = swap(banded, ("x",))
-    other = lax.ppermute(own, "c", ((0, 1), (1, 0)))
-    first_row = (2 * chip + core) * 32
-    return gram(first_row.reshape(1), own, other)
+    own, send = gram(place, swap(banded, ("x",)))
+    return add(place, own, lax.all_gather(send, "c", axis=0, tiled=False))
 
 
 def solution(mesh):

time: 116 us -> 109 us (0.940)
  starting transfers between devices: 6.64 us -> 0 us
  blocking collectives: 92.8 us -> 98.1 us
  waiting for transfers between devices: 2.26 us -> 0 us
  local copies, waits for them, and re-layouts: 2.36 us -> 0.12 us
  Pallas kernels: 11.5 us -> 9.42 us
    all_gather x1 -> x2, blocking collectives: 5.52 us -> 12.2 us  [the longest x1 6.53 us: shards(): return add(place, own, lax.all_gather(send, 'c', axis=0, tiled=False))]
    ppermute x1 -> x0, starting transfers between devices: 6.64 us -> none  [shards(): other = lax.ppermute(own, 'c', ((0, 1), (1, 0)))]
    pallas_call x1, Pallas kernels: 8.5 us -> 3.41 us  [kerr_step(): pl.pallas_call(kerr_kernel, out_shape=jax.ShapeDtypeStruct((NDEV, 16, 128...]
    pallas_call x2 -> x3, Pallas kernels: 2.3 us -> 5.32 us  [the longest x1 2.66 us: pack(): pl.pallas_call(pack_kernel, out_shape=jax.ShapeDtypeStruct((NDEV, 9, 4, 1...]
    unnamed x12 -> x8, local copies, waits for them, and re-layouts: 2.34 us -> 0.02 us
    ppermute x1 -> x0, waiting for transfers between devices: 2.26 us -> none  [shards(): other = lax.ppermute(own, 'c', ((0, 1), (1, 0)))]
    all_to_all x4, blocking collectives: 87.3 us -> 86 us  [swap(): return lax.all_to_all(array, axes, split_axis=0, concat_axis=0, tiled=True)]
  transfers between devices with their start and end apart: 1 -> 0, of which waited for: 1 -> 0; matrix products, arithmetic and copies ran while one was open for 0% -> 0% of each run, Pallas kernels for 0% -> 0%
where the time goes in v2:
time: 109 us; the launch traced here: 108 us
  blocking collectives  98.1 us (90%)
  Pallas kernels  9.42 us (9%)
    all_to_all x4, blocking collectives, swap(): return lax.all_to_all(array, axes, split_axis=0, concat_axis=0, tiled=True)  86 us
    all_gather x1, blocking collectives, shards(): return add(place, own, lax.all_gather(send, 'c', axis=0, tiled=False))  6.53 us
    all_gather x1, blocking collectives, shards(): coeff = lax.all_gather(halves, 'c', axis=0, tiled=False)  5.65 us
    pallas_call x1, Pallas kernels, kerr_step(): pl.pallas_call(kerr_kernel, out_shape=jax.ShapeDtypeStruct((NDEV, 16, 128...  3.41 us
    pallas_call x1, Pallas kernels, pack(): pl.pallas_call(pack_kernel, out_shape=jax.ShapeDtypeStruct((NDEV, 9, 4, 1...  2.66 us

profile of v2, /device:TPU:1, one launch (start us, length us, event | category | flops | bytes accessed | tf_op | source)
XLA Modules:
  0.0 108.4 jit_solution(1089580233240385691)
XLA Ops:
  0.0 0.6 pad_add_fusion.place_ref
  0.6 2.7 %pack.1 = bf16[64,9,4,128]{3,2,1,0:T(4,128)(2,1)} custom-call(s32[3]{0:T(128)} %pad_add_fusion.place_ref, s32[1,4]{1,0:T(1,128)} %list_ref.1, bf16[2,1,4,16384]{3,2,1,0:T(4,128)(2,1)} %field_hbm.1, bf16[1,64,64]{2,1,0:T(8,128)(2,1)} %coeff_hbm.1), custom_call_target="tpu_custom_call" | custom-call | tf_op jit(solution)/shard_map/pack/pallas_call | solution.py:76
  3.3 34.6 %all_to_all.20.data_ref = bf16[64,9,4,128]{3,2,1,0:T(4,128)(2,1)S(1)} all-to-all(bf16[64,9,4,128]{3,2,1,0:T(4,128)(2,1)} %pack.1), channel_id=1, replica_groups=mesh['y'=8,'z'=8,'x'=4,'c'=2] {'y','z'}, dimensions={0} | all-to-all | bytes 1179648 | tf_op jit(solution)/shard_map/all_to_all | solution.py:326
  38.0 0.1 slice.4
  38.1 5.7 %all_gather.9.coeff_ref = bf16[2,64,16,128]{3,2,1,0:T(8,128)(2,1)S(1)} all-gather(bf16[1,64,16,128]{3,2,1,0:T(8,128)(2,1)S(1)} %bitcast.6), channel_id=1, replica_groups=mesh['y'=8,'z'=8,'x'=4,'c'=2] {'c'}, dimensions={0}, use_global_device_ids=true | all-gather | bytes 786432 | tf_op jit(solution)/shard_map/all_gather | solution.py:333
  43.7 3.4 %kerr.1 = bf16[64,16,128]{2,1,0:T(8,128)(2,1)S(1)} custom-call(bf16[64,9,4,128]{3,2,1,0:T(4,128)(2,1)S(1)} %all_to_all.20.data_ref, bf16[2,64,16,128]{3,2,1,0:T(8,128)(2,1)S(1)} %all_gather.9.coeff_ref), custom_call_target="tpu_custom_call" | custom-call | tf_op jit(solution)/shard_map/kerr/pallas_call | solution.py:161
  47.1 0.0 copy-start
  47.1 0.0 copy-start.1
  47.1 0.0 copy-start.2
  47.2 18.3 %all_to_all.21.data_ref = bf16[64,16,128]{2,1,0:T(8,128)(2,1)S(1)} all-to-all(bf16[64,16,128]{2,1,0:T(8,128)(2,1)S(1)} %kerr.1), channel_id=1, replica_groups=mesh['y'=8,'z'=8,'x'=4,'c'=2] {'y','z'}, dimensions={0} | all-to-all | bytes 524288 | tf_op jit(solution)/shard_map/all_to_all | solution.py:326
  65.5 0.0 copy-done
  65.5 0.0 copy-done.1
  65.5 0.0 copy-done.2
  65.5 0.6 dft.1
  66.1 17.9 %all_to_all.22.data_ref = bf16[64,16,128]{2,1,0:T(8,128)(2,1)S(1)} all-to-all(bf16[64,16,128]{2,1,0:T(8,128)(2,1)S(1)} %dft.1), channel_id=1, replica_groups=mesh['y'=8,'z'=8,'x'=4,'c'=2] {'y','z'}, dimensions={0} | all-to-all | bytes 524288 | tf_op jit(solution)/shard_map/all_to_all | solution.py:326
  84.0 0.1 order.1
  84.1 0.0 copy-start.3
  84.1 15.1 %all_to_all.23.data_ref = bf16[4,2,2,256,128]{4,3,2,1,0:T(8,128)(2,1)S(1)} all-to-all(bf16[4,2,2,256,128]{4,3,2,1,0:T(8,128)(2,1)S(1)} %order.1), channel_id=1, replica_groups=mesh['y'=8,'z'=8,'x'=4,'c'=2] {'x'}, dimensions={0} | all-to-all | bytes 2097152 | tf_op jit(solution)/shard_map/all_to_all | solution.py:326
  99.2 0.0 copy-done.3
  99.2 1.3 %gram.1 = (f32[8,2,32,256]{3,2,1,0:T(8,128)S(1)}, bf16[8,2,32,256]{3,2,1,0:T(8,128)(2,1)S(1)}) custom-call(s32[3]{0:T(128)S(1)} %copy-done.3, bf16[4,2,2,256,128]{4,3,2,1,0:T(8,128)(2,1)S(1)} %all_to_all.23.data_ref), custom_call_target="tpu_custom_call" | custom-call | tf_op jit(solution)/shard_map/gram/pallas_call | solution.py:297
  100.5 6.5 %all-gather = bf16[16,2,32,256]{3,2,1,0:T(8,128)(2,1)S(1)} all-gather(bf16[8,2,32,256]{3,2,1,0:T(8,128)(2,1)S(1)} %get-tuple-element.8), channel_id=2, replica_groups=mesh['y'=8,'z'=8,'x'=4,'c'=2] {'c'}, dimensions={0}, use_global_device_ids=true | all-gather | bytes 786432 | tf_op jit(solution)/shard_map/all_gather | solution.py:338
  107.0 1.4 %add.9 = f32[8,2,32,256]{3,2,1,0:T(8,128)} custom-call(s32[3]{0:T(128)S(1)} %copy-done.3, f32[8,2,32,256]{3,2,1,0:T(8,128)S(1)} %get-tuple-element.7.own_ref, bf16[2,8,2,32,256]{4,3,2,1,0:T(8,128)(2,1)S(1)} %bitcast.5), custom_call_target="tpu_custom_call" | custom-call | tf_op jit(solution)/shard_map/add/pallas_call | solution.py:315
Async XLA Ops:
  47.1 18.4 %copy-start = (f32[2,128,128]{2,1,0:T(8,128)S(1)}, f32[2,128,128]{2,1,0:T(8,128)}, u32[]{:S(2)}) copy-start(f32[2,128,128]{2,1,0:T(8,128)} %constant.26.clone.twist_ref) | copy-start | bytes 393220
  47.1 18.3 %copy-start.1 = (bf16[256,256]{1,0:T(8,128)(2,1)S(1)}, bf16[256,256]{1,0:T(8,128)(2,1)}, u32[]{:S(2)}) copy-start(bf16[256,256]{1,0:T(8,128)(2,1)} %constant.25.clone.second_ref) | copy-start | bytes 393220
  47.1 18.3 %copy-start.2 = (bf16[256,256]{1,0:T(8,128)(2,1)S(1)}, bf16[256,256]{1,0:T(8,128)(2,1)}, u32[]{:S(2)}) copy-start(bf16[256,256]{1,0:T(8,128)(2,1)} %constant.24.clone.first_ref) | copy-start | bytes 393220
  84.1 15.2 %copy-start.3 = (s32[3]{0:T(128)S(1)}, s32[3]{0:T(128)}, u32[]{:S(2)}) copy-start(s32[3]{0:T(128)} %pad_add_fusion.place_ref) | copy-start | bytes 40

commit v3 on v2

--- a/solution.py
+++ b/solution.py
@@ -12,6 +12,8 @@
 MB = 8
 FT = 128
 FB = 32
+NT = 16384
+PACK_PARTS = 4
 NMB = 32
 NBLK = 64
 MODES = 256
@@ -37,55 +39,74 @@
     return pl.BlockSpec(memory_space=pltpu.HBM)
 
 
-def in_smem():
-    return pl.BlockSpec(memory_space=pltpu.SMEM)
-
-
-def pack_kernel(place_ref, list_ref, field_hbm, coeff_hbm, out_ref, field, coeff, sems):
-    field_copy = pltpu.make_async_copy(field_hbm, field, sems.at[0])
-    coeff_copy = pltpu.make_async_copy(coeff_hbm, coeff, sems.at[1])
-    field_copy.start()
+def pack_kernel(list_hbm, field_hbm, coeff_hbm, out_hbm, listed, field, coeff, out, sems, out_sems):
+    coeff_copy = pltpu.make_async_copy(coeff_hbm, coeff, sems.at[0])
+    list_copy = pltpu.make_async_copy(list_hbm, listed, sems.at[1])
     coeff_copy.start()
-    core = place_ref[0]
+    list_copy.start()
+    field_copies = []
+    for g in range(PACK_PARTS):
+        times = pl.ds(g * (NT // PACK_PARTS), NT // PACK_PARTS)
+        field_copies.append(
+            pltpu.make_async_copy(
+                field_hbm.at[:, :, :, times], field.at[:, :, :, times], sems.at[2 + g]
+            )
+        )
+        field_copies[g].start()
+    core = lax.axis_index("c")
+    place = lax.axis_index(MODE)
     row = lax.broadcasted_iota(jnp.int32, (32, 64), 0) + 32 * core
     col = lax.broadcasted_iota(jnp.int32, (32, 64), 1)
     pick = (col == (row % MB) * MB + row // MB).astype(F32).astype(BF16)
     lane = lax.broadcasted_iota(jnp.int32, (4, 128), 1)
     line = lax.broadcasted_iota(jnp.int32, (4, 128), 0)
-    index = jnp.zeros((4, 128), jnp.int32)
-    for j in range(4):
-        index = jnp.where((lane == place_ref[1]) & (line == j), list_ref[0, j], index)
-    index = index.astype(F32).astype(BF16)
     coeff_copy.wait()
     own = jnp.dot(pick, coeff[0], preferred_element_type=F32)
     own = jnp.concatenate([own[:16], own[16:]], axis=1).astype(BF16)
-    for i in range(NDEV):
-        for q in range(4):
-            out_ref[i, 4 + q] = own[4 * q : 4 * q + 4]
-        out_ref[i, 8] = index
-    field_copy.wait()
-    for i in range(NDEV):
-        for tt in range(2):
-            for part in range(2):
-                out_ref[i, 2 * tt + part] = field[
-                    part, 0, :, (2 * i + tt) * 128 : (2 * i + tt) * 128 + 128
-                ]
-
-
-def pack(place, block_list, field, coeff):
+    list_copy.wait()
+    index = jnp.zeros((4, 128), jnp.int32)
+    for j in range(4):
+        index = jnp.where((lane == place) & (line == j), listed[0, j], index)
+    index = index.astype(F32).astype(BF16)
+    each = NDEV // PACK_PARTS
+    out_copies = []
+    for g in range(PACK_PARTS):
+        field_copies[g].wait()
+        for i in range(g * each, g * each + each):
+            for tt in range(2):
+                for part in range(2):
+                    at = (2 * i + tt) * 128
+                    out[i, 2 * tt + part] = field[part, 0, :, at : at + 128]
+            for q in range(4):
+                out[i, 4 + q] = own[4 * q : 4 * q + 4]
+            out[i, 8] = index
+        receivers = pl.ds(g * each, each)
+        out_copies.append(
+            pltpu.make_async_copy(out.at[receivers], out_hbm.at[receivers], out_sems.at[g])
+        )
+        out_copies[g].start()
+    for copy in out_copies:
+        copy.wait()
+
+
+def pack(block_list, field, coeff):
+    shape = (NDEV, 9, 4, 128)
     return pl.pallas_call(
         pack_kernel,
-        out_shape=jax.ShapeDtypeStruct((NDEV, 9, 4, 128), BF16),
-        in_specs=[in_smem(), in_smem(), in_hbm(), in_hbm()],
-        out_specs=in_vmem(),
+        out_shape=jax.ShapeDtypeStruct(shape, BF16),
+        in_specs=[in_hbm(), in_hbm(), in_hbm()],
+        out_specs=in_hbm(),
         scratch_shapes=[
+            pltpu.SMEM(block_list.shape, jnp.int32),
             pltpu.VMEM(field.shape, BF16),
             pltpu.VMEM(coeff.shape, BF16),
-            pltpu.SemaphoreType.DMA((2,)),
+            pltpu.VMEM(shape, BF16),
+            pltpu.SemaphoreType.DMA((2 + PACK_PARTS,)),
+            pltpu.SemaphoreType.DMA((PACK_PARTS,)),
         ],
         compiler_params=params(60 * 2**20),
         name="pack",
-    )(place, block_list, field, coeff)
+    )(block_list, field, coeff)
 
 
 def kerr_kernel(data_ref, coeff_ref, out_ref, field, total, listed, indices, sem):
@@ -262,10 +283,11 @@
     )(data)
 
 
-def gram_kernel(place_ref, data_ref, own_ref, send_ref):
-    core = place_ref[0]
-    keep = pl.multiple_of(64 * place_ref[2] + 32 * core, 32)
-    give = pl.multiple_of(64 * place_ref[2] + 32 * (1 - core), 32)
+def gram_kernel(data_ref, own_ref, send_ref):
+    core = lax.axis_index("c")
+    chip = lax.axis_index("x")
+    keep = pl.multiple_of(64 * chip + 32 * core, 32)
+    give = pl.multiple_of(64 * chip + 32 * (1 - core), 32)
     lane = lax.broadcasted_iota(jnp.int32, (32, 128), 1) // FB
     for h in range(2):
         lefts = [[] for _ in range(16)]
@@ -293,33 +315,42 @@
                 send_ref[4 * h + band, d] = result[256 + at : 256 + at + 32].astype(BF16)
 
 
-def gram(place, data):
+def gram(data):
     return pl.pallas_call(
         gram_kernel,
         out_shape=(
             jax.ShapeDtypeStruct((8, 2, 32, MODES), F32),
             jax.ShapeDtypeStruct((8, 2, 32, MODES), BF16),
         ),
-        in_specs=[in_smem(), in_vmem()],
+        in_specs=[in_vmem()],
         out_specs=(in_vmem(), in_vmem()),
         compiler_params=params(),
         name="gram",
-    )(place, data)
-
-
-def add_kernel(place_ref, own_ref, sent_ref, out_ref):
-    out_ref[...] = own_ref[...] + sent_ref[1 - place_ref[0]].astype(F32)
-
-
-def add(place, own, sent):
+    )(data)
+
+
+def add_kernel(own_ref, sent_ref, out_hbm, out, sems):
+    other = 1 - lax.axis_index("c")
+    copies = []
+    for b in range(4):
+        bands = pl.ds(2 * b, 2)
+        out[bands] = own_ref[bands] + sent_ref[other, bands].astype(F32)
+        copies.append(pltpu.make_async_copy(out.at[bands], out_hbm.at[bands], sems.at[b]))
+        copies[b].start()
+    for copy in copies:
+        copy.wait()
+
+
+def add(own, sent):
     return pl.pallas_call(
         add_kernel,
-        out_shape=jax.ShapeDtypeStruct((8, 2, 32, MODES), F32),
-        in_specs=[in_smem(), in_vmem(), in_vmem()],
-        out_specs=in_vmem(),
+        out_shape=jax.ShapeDtypeStruct(own.shape, F32),
+        in_specs=[in_vmem(), in_vmem()],
+        out_specs=in_hbm(),
+        scratch_shapes=[pltpu.VMEM(own.shape, F32), pltpu.SemaphoreType.DMA((4,))],
         compiler_params=params(),
         name="add",
-    )(place, own, sent)
+    )(own, sent)
 
 
 def swap(array, axes):
@@ -327,15 +358,14 @@
 
 
 def shards(input_field, kerr_coeff, block_list):
-    place = jnp.stack([lax.axis_index("c"), lax.axis_index(MODE), lax.axis_index("x")])
-    timed = swap(pack(place, block_list, input_field, kerr_coeff), MODE)
+    timed = swap(pack(block_list, input_field, kerr_coeff), MODE)
     halves = timed[:, 4:8].reshape(NDEV, 16, 128)
     coeff = lax.all_gather(halves, "c", axis=0, tiled=False)
     stepped = kerr_step(timed, coeff)
     spectrum = transform(swap(stepped, MODE))
     banded = order(swap(spectrum, MODE))
-    own, send = gram(place, swap(banded, ("x",)))
-    return add(place, own, lax.all_gather(send, "c", axis=0, tiled=False))
+    own, send = gram(swap(banded, ("x",)))
+    return add(own, lax.all_gather(send, "c", axis=0, tiled=False))
 
 
 def solution(mesh):

time: 109 us -> 106 us (0.972)
  Pallas kernels: 9.42 us -> 7.54 us
    pallas_call x2, Pallas kernels: 4.04 us -> 2.7 us  [the longest x1 1.87 us: pack(): pl.pallas_call(pack_kernel, out_shape=jax.ShapeDtypeStruct(shape, BF16),...]
where the time goes in v3:
time: 106 us
  blocking collectives  98.2 us (93%)
  Pallas kernels  7.54 us (7%)
    all_to_all x4, blocking collectives, swap(): return lax.all_to_all(array, axes, split_axis=0, concat_axis=0, tiled=True)  86 us
    all_gather x1, blocking collectives, shards(): return add(own, lax.all_gather(send, 'c', axis=0, tiled=False))  6.52 us
    all_gather x1, blocking collectives, shards(): coeff = lax.all_gather(halves, 'c', axis=0, tiled=False)  5.65 us
    pallas_call x1, Pallas kernels, kerr_step(): pl.pallas_call(kerr_kernel, out_shape=jax.ShapeDtypeStruct((NDEV, 16, 128...  3.41 us

profile of v3, /device:TPU:1, one launch (start us, length us, event | category | flops | bytes accessed | tf_op | source)
XLA Modules:
  0.0 105.9 jit_solution(6639698393326507167)
XLA Ops:
  0.0 1.9 %pack.1 = bf16[64,9,4,128]{3,2,1,0:T(4,128)(2,1)} custom-call(s32[1,4]{1,0:T(1,128)} %list_hbm.1, bf16[2,1,4,16384]{3,2,1,0:T(4,128)(2,1)} %field_hbm.1, bf16[1,64,64]{2,1,0:T(8,128)(2,1)} %coeff_hbm.1), custom_call_target="tpu_custom_call" | custom-call | tf_op jit(solution)/shard_map/pack/pallas_call | solution.py:94
  1.9 34.6 %all_to_all.20.data_ref = bf16[64,9,4,128]{3,2,1,0:T(4,128)(2,1)S(1)} all-to-all(bf16[64,9,4,128]{3,2,1,0:T(4,128)(2,1)} %pack.1), channel_id=1, replica_groups=mesh['y'=8,'z'=8,'x'=4,'c'=2] {'y','z'}, dimensions={0} | all-to-all | bytes 1179648 | tf_op jit(solution)/shard_map/all_to_all | solution.py:357
  36.5 0.1 slice.4
  36.6 5.7 %all_gather.9.coeff_ref = bf16[2,64,16,128]{3,2,1,0:T(8,128)(2,1)S(1)} all-gather(bf16[1,64,16,128]{3,2,1,0:T(8,128)(2,1)S(1)} %bitcast.3), channel_id=1, replica_groups=mesh['y'=8,'z'=8,'x'=4,'c'=2] {'c'}, dimensions={0}, use_global_device_ids=true | all-gather | bytes 786432 | tf_op jit(solution)/shard_map/all_gather | solution.py:363
  42.3 3.4 %kerr.1 = bf16[64,16,128]{2,1,0:T(8,128)(2,1)S(1)} custom-call(bf16[64,9,4,128]{3,2,1,0:T(4,128)(2,1)S(1)} %all_to_all.20.data_ref, bf16[2,64,16,128]{3,2,1,0:T(8,128)(2,1)S(1)} %all_gather.9.coeff_ref), custom_call_target="tpu_custom_call" | custom-call | tf_op jit(solution)/shard_map/kerr/pallas_call | solution.py:182
  45.7 0.0 copy-start
  45.7 0.0 copy-start.1
  45.7 0.0 copy-start.2
  45.7 18.3 %all_to_all.21.data_ref = bf16[64,16,128]{2,1,0:T(8,128)(2,1)S(1)} all-to-all(bf16[64,16,128]{2,1,0:T(8,128)(2,1)S(1)} %kerr.1), channel_id=1, replica_groups=mesh['y'=8,'z'=8,'x'=4,'c'=2] {'y','z'}, dimensions={0} | all-to-all | bytes 524288 | tf_op jit(solution)/shard_map/all_to_all | solution.py:357
  64.1 0.0 copy-done
  64.1 0.0 copy-done.1
  64.1 0.0 copy-done.2
  64.1 0.6 dft.1
  64.7 17.8 %all_to_all.22.data_ref = bf16[64,16,128]{2,1,0:T(8,128)(2,1)S(1)} all-to-all(bf16[64,16,128]{2,1,0:T(8,128)(2,1)S(1)} %dft.1), channel_id=1, replica_groups=mesh['y'=8,'z'=8,'x'=4,'c'=2] {'y','z'}, dimensions={0} | all-to-all | bytes 524288 | tf_op jit(solution)/shard_map/all_to_all | solution.py:357
  82.5 0.1 order.1
  82.6 15.2 %all_to_all.23.data_ref = bf16[4,2,2,256,128]{4,3,2,1,0:T(8,128)(2,1)S(1)} all-to-all(bf16[4,2,2,256,128]{4,3,2,1,0:T(8,128)(2,1)S(1)} %order.1), channel_id=1, replica_groups=mesh['y'=8,'z'=8,'x'=4,'c'=2] {'x'}, dimensions={0} | all-to-all | bytes 2097152 | tf_op jit(solution)/shard_map/all_to_all | solution.py:357
  97.8 0.7 gram.1
  98.5 6.5 %all-gather = bf16[16,2,32,256]{3,2,1,0:T(8,128)(2,1)S(1)} all-gather(bf16[8,2,32,256]{3,2,1,0:T(8,128)(2,1)S(1)} %get-tuple-element.8), channel_id=2, replica_groups=mesh['y'=8,'z'=8,'x'=4,'c'=2] {'c'}, dimensions={0}, use_global_device_ids=true | all-gather | bytes 786432 | tf_op jit(solution)/shard_map/all_gather | solution.py:368
  105.1 0.8 add.1
Async XLA Ops:
  45.7 18.4 %copy-start = (f32[2,128,128]{2,1,0:T(8,128)S(1)}, f32[2,128,128]{2,1,0:T(8,128)}, u32[]{:S(2)}) copy-start(f32[2,128,128]{2,1,0:T(8,128)} %constant.8.clone.twist_ref) | copy-start | bytes 393220
  45.7 18.4 %copy-start.1 = (bf16[256,256]{1,0:T(8,128)(2,1)S(1)}, bf16[256,256]{1,0:T(8,128)(2,1)}, u32[]{:S(2)}) copy-start(bf16[256,256]{1,0:T(8,128)(2,1)} %constant.7.clone.second_ref) | copy-start | bytes 393220
  45.7 18.4 %copy-start.2 = (bf16[256,256]{1,0:T(8,128)(2,1)S(1)}, bf16[256,256]{1,0:T(8,128)(2,1)}, u32[]{:S(2)}) copy-start(bf16[256,256]{1,0:T(8,128)(2,1)} %constant.6.clone.first_ref) | copy-start | bytes 393220

commit v4 on v3

--- a/solution.py
+++ b/solution.py
@@ -58,15 +58,16 @@
     row = lax.broadcasted_iota(jnp.int32, (32, 64), 0) + 32 * core
     col = lax.broadcasted_iota(jnp.int32, (32, 64), 1)
     pick = (col == (row % MB) * MB + row // MB).astype(F32).astype(BF16)
-    lane = lax.broadcasted_iota(jnp.int32, (4, 128), 1)
-    line = lax.broadcasted_iota(jnp.int32, (4, 128), 0)
+    lane = lax.broadcasted_iota(jnp.int32, (2, 128), 1)
+    line = lax.broadcasted_iota(jnp.int32, (2, 128), 0)
     coeff_copy.wait()
     own = jnp.dot(pick, coeff[0], preferred_element_type=F32)
     own = jnp.concatenate([own[:16], own[16:]], axis=1).astype(BF16)
     list_copy.wait()
-    index = jnp.zeros((4, 128), jnp.int32)
+    index = jnp.zeros((2, 128), jnp.int32)
     for j in range(4):
-        index = jnp.where((lane == place) & (line == j), listed[0, j], index)
+        here = (lane == place + 64 * (j % 2)) & (line == j // 2)
+        index = jnp.where(here, listed[0, j], index)
     index = index.astype(F32).astype(BF16)
     each = NDEV // PACK_PARTS
     out_copies = []
@@ -76,10 +77,12 @@
             for tt in range(2):
                 for part in range(2):
                     at = (2 * i + tt) * 128
-                    out[i, 2 * tt + part] = field[part, 0, :, at : at + 128]
-            for q in range(4):
-                out[i, 4 + q] = own[4 * q : 4 * q + 4]
-            out[i, 8] = index
+                    tile = field[part, 0, :, at : at + 128]
+                    out[i, 4 * tt + 2 * part] = tile[0:2]
+                    out[i, 4 * tt + 2 * part + 1] = tile[2:4]
+            for q in range(8):
+                out[i, 8 + q] = own[2 * q : 2 * q + 2]
+            out[i, 16] = index
         receivers = pl.ds(g * each, each)
         out_copies.append(
             pltpu.make_async_copy(out.at[receivers], out_hbm.at[receivers], out_sems.at[g])
@@ -90,7 +93,7 @@
 
 
 def pack(block_list, field, coeff):
-    shape = (NDEV, 9, 4, 128)
+    shape = (NDEV, 17, 2, 128)
     return pl.pallas_call(
         pack_kernel,
         out_shape=jax.ShapeDtypeStruct(shape, BF16),
@@ -109,30 +112,28 @@
     )(block_list, field, coeff)
 
 
-def kerr_kernel(data_ref, coeff_ref, out_ref, field, total, listed, indices, sem):
-    index = jnp.sum(data_ref[:, 8].astype(F32), axis=0)
-    listed[...] = jnp.concatenate([index, index], axis=0).astype(jnp.int32)
-    list_copy = pltpu.make_async_copy(listed, indices, sem)
-    list_copy.start()
+def kerr_kernel(data_ref, coeff_ref, out_ref, field, total):
+    index = jnp.sum(data_ref[:, 16].astype(F32), axis=0).astype(jnp.int32)
     for b in range(NMB):
         for tt in range(2):
             for part in range(2):
+                at = 4 * tt + 2 * part
                 both = jnp.concatenate(
                     [
-                        data_ref[2 * b, 2 * tt + part].astype(F32),
-                        data_ref[2 * b + 1, 2 * tt + part].astype(F32),
+                        data_ref[2 * b + s, at + h].astype(F32)
+                        for s in range(2)
+                        for h in range(2)
                     ],
                     axis=0,
                 )
                 field[part, b, :, tt * 128 : tt * 128 + 128] = both
                 total[part, b, :, tt * 128 : tt * 128 + 128] = both
-    list_copy.wait()
-
-    def one_block(k, carry):
-        at_p = indices[0, k]
-        at_l = indices[1, k]
-        at_m = indices[2, k]
-        at_n = indices[3, k]
+
+    for k in range(NBLK):
+        at_p = index[0, k]
+        at_l = index[0, 64 + k]
+        at_m = index[1, k]
+        at_n = index[1, 64 + k]
         n_re = field[0, at_n]
         n_im = field[1, at_n]
         pair_re = []
@@ -162,9 +163,6 @@
             term_im = term_im + (w_re * l_im + w_im * l_re)
         total[0, at_p] -= kerr_strength * term_im
         total[1, at_p] += kerr_strength * term_re
-        return carry
-
-    lax.fori_loop(0, NBLK, one_block, 0, unroll=16)
 
     for b in range(NMB):
         new = (total[0, b], total[1, b])
@@ -187,9 +185,6 @@
         scratch_shapes=[
             pltpu.VMEM((2, NMB, MB, 256), F32),
             pltpu.VMEM((2, NMB, MB, 256), F32),
-            pltpu.VMEM((8, 128), jnp.int32),
-            pltpu.SMEM((8, 128), jnp.int32),
-            pltpu.SemaphoreType.DMA,
         ],
         compiler_params=params(),
         name="kerr",
@@ -359,7 +354,7 @@
 
 def shards(input_field, kerr_coeff, block_list):
     timed = swap(pack(block_list, input_field, kerr_coeff), MODE)
-    halves = timed[:, 4:8].reshape(NDEV, 16, 128)
+    halves = timed[:, 8:16].reshape(NDEV, 16, 128)
     coeff = lax.all_gather(halves, "c", axis=0, tiled=False)
     stepped = kerr_step(timed, coeff)
     spectrum = transform(swap(stepped, MODE))

time: 106 us -> 106 us (level)
  no operation moved by 1% of the time
where the time goes in v4:
time: 106 us; the launch traced here: 105 us
  blocking collectives  97.4 us (92%)
  Pallas kernels  7.44 us (7%)
    all_to_all x4, blocking collectives, swap(): return lax.all_to_all(array, axes, split_axis=0, concat_axis=0, tiled=True)  85.2 us
    all_gather x1, blocking collectives, shards(): return add(own, lax.all_gather(send, 'c', axis=0, tiled=False))  6.55 us
    all_gather x1, blocking collectives, shards(): coeff = lax.all_gather(halves, 'c', axis=0, tiled=False)  5.65 us
    pallas_call x1, Pallas kernels, kerr_step(): pl.pallas_call(kerr_kernel, out_shape=jax.ShapeDtypeStruct((NDEV, 16, 128...  3.22 us

profile of v4, /device:TPU:1, one launch (start us, length us, event | category | flops | bytes accessed | tf_op | source)
XLA Modules:
  0.0 105.1 jit_solution(12293657521499502072)
XLA Ops:
  0.0 2.0 %pack.1 = bf16[64,17,2,128]{3,2,1,0:T(2,128)(2,1)} custom-call(s32[1,4]{1,0:T(1,128)} %list_hbm.1, bf16[2,1,4,16384]{3,2,1,0:T(4,128)(2,1)} %field_hbm.1, bf16[1,64,64]{2,1,0:T(8,128)(2,1)} %coeff_hbm.1), custom_call_target="tpu_custom_call" | custom-call | tf_op jit(solution)/shard_map/pack/pallas_call | solution.py:97
  2.0 34.0 %all_to_all.20.data_ref = bf16[64,17,2,128]{3,2,1,0:T(2,128)(2,1)S(1)} all-to-all(bf16[64,17,2,128]{3,2,1,0:T(2,128)(2,1)} %pack.1), channel_id=1, replica_groups=mesh['y'=8,'z'=8,'x'=4,'c'=2] {'y','z'}, dimensions={0} | all-to-all | bytes 1114112 | tf_op jit(solution)/shard_map/all_to_all | solution.py:352
  36.0 0.2 slice.4
  36.2 5.6 %all_gather.9.coeff_ref = bf16[2,64,16,128]{3,2,1,0:T(8,128)(2,1)S(1)} all-gather(bf16[1,64,16,128]{3,2,1,0:T(8,128)(2,1)S(1)} %bitcast.3), channel_id=1, replica_groups=mesh['y'=8,'z'=8,'x'=4,'c'=2] {'c'}, dimensions={0}, use_global_device_ids=true | all-gather | bytes 786432 | tf_op jit(solution)/shard_map/all_gather | solution.py:358
  41.8 3.2 %kerr.1 = bf16[64,16,128]{2,1,0:T(8,128)(2,1)S(1)} custom-call(bf16[64,17,2,128]{3,2,1,0:T(2,128)(2,1)S(1)} %all_to_all.20.data_ref, bf16[2,64,16,128]{3,2,1,0:T(8,128)(2,1)S(1)} %all_gather.9.coeff_ref), custom_call_target="tpu_custom_call" | custom-call | tf_op jit(solution)/shard_map/kerr/pallas_call | solution.py:180
  45.1 0.0 copy-start
  45.1 0.0 copy-start.1
  45.1 0.0 copy-start.2
  45.1 18.2 %all_to_all.21.data_ref = bf16[64,16,128]{2,1,0:T(8,128)(2,1)S(1)} all-to-all(bf16[64,16,128]{2,1,0:T(8,128)(2,1)S(1)} %kerr.1), channel_id=1, replica_groups=mesh['y'=8,'z'=8,'x'=4,'c'=2] {'y','z'}, dimensions={0} | all-to-all | bytes 524288 | tf_op jit(solution)/shard_map/all_to_all | solution.py:352
  63.3 0.0 copy-done
  63.3 0.0 copy-done.1
  63.3 0.0 copy-done.2
  63.3 0.6 dft.1
  63.9 17.8 %all_to_all.22.data_ref = bf16[64,16,128]{2,1,0:T(8,128)(2,1)S(1)} all-to-all(bf16[64,16,128]{2,1,0:T(8,128)(2,1)S(1)} %dft.1), channel_id=1, replica_groups=mesh['y'=8,'z'=8,'x'=4,'c'=2] {'y','z'}, dimensions={0} | all-to-all | bytes 524288 | tf_op jit(solution)/shard_map/all_to_all | solution.py:352
  81.8 0.1 order.1
  81.9 15.1 %all_to_all.23.data_ref = bf16[4,2,2,256,128]{4,3,2,1,0:T(8,128)(2,1)S(1)} all-to-all(bf16[4,2,2,256,128]{4,3,2,1,0:T(8,128)(2,1)S(1)} %order.1), channel_id=1, replica_groups=mesh['y'=8,'z'=8,'x'=4,'c'=2] {'x'}, dimensions={0} | all-to-all | bytes 2097152 | tf_op jit(solution)/shard_map/all_to_all | solution.py:352
  97.0 0.7 gram.1
  97.8 6.5 %all-gather = bf16[16,2,32,256]{3,2,1,0:T(8,128)(2,1)S(1)} all-gather(bf16[8,2,32,256]{3,2,1,0:T(8,128)(2,1)S(1)} %get-tuple-element.8), channel_id=2, replica_groups=mesh['y'=8,'z'=8,'x'=4,'c'=2] {'c'}, dimensions={0}, use_global_device_ids=true | all-gather | bytes 786432 | tf_op jit(solution)/shard_map/all_gather | solution.py:363
  104.3 0.8 add.1
Async XLA Ops:
  45.1 18.3 %copy-start = (f32[2,128,128]{2,1,0:T(8,128)S(1)}, f32[2,128,128]{2,1,0:T(8,128)}, u32[]{:S(2)}) copy-start(f32[2,128,128]{2,1,0:T(8,128)} %constant.8.clone.twist_ref) | copy-start | bytes 393220
  45.1 18.3 %copy-start.1 = (bf16[256,256]{1,0:T(8,128)(2,1)S(1)}, bf16[256,256]{1,0:T(8,128)(2,1)}, u32[]{:S(2)}) copy-start(bf16[256,256]{1,0:T(8,128)(2,1)} %constant.7.clone.second_ref) | copy-start | bytes 393220
  45.1 18.2 %copy-start.2 = (bf16[256,256]{1,0:T(8,128)(2,1)S(1)}, bf16[256,256]{1,0:T(8,128)(2,1)}, u32[]{:S(2)}) copy-start(bf16[256,256]{1,0:T(8,128)(2,1)} %constant.6.clone.first_ref) | copy-start | bytes 393220

commit v5 on v4

--- a/solution.py
+++ b/solution.py
@@ -112,10 +112,11 @@
     )(block_list, field, coeff)
 
 
-def kerr_kernel(data_ref, coeff_ref, out_ref, field, total):
+def kerr_kernel(data_ref, coeff_ref, out_ref, spread, twice, total):
     index = jnp.sum(data_ref[:, 16].astype(F32), axis=0).astype(jnp.int32)
     for b in range(NMB):
         for tt in range(2):
+            times = slice(tt * 128, tt * 128 + 128)
             for part in range(2):
                 at = 4 * tt + 2 * part
                 both = jnp.concatenate(
@@ -126,43 +127,55 @@
                     ],
                     axis=0,
                 )
-                field[part, b, :, tt * 128 : tt * 128 + 128] = both
-                total[part, b, :, tt * 128 : tt * 128 + 128] = both
+                total[part, b, :, times] = both
+                twice[part, b, :, times] = jnp.concatenate([both, both], axis=0).astype(BF16)
+                for j in range(4):
+                    spread[part, b, j, :, times] = jnp.concatenate(
+                        [
+                            jnp.broadcast_to(both[2 * j + h : 2 * j + h + 1], (8, 128))
+                            for h in range(2)
+                        ],
+                        axis=0,
+                    ).astype(BF16)
 
     for k in range(NBLK):
         at_p = index[0, k]
         at_l = index[0, 64 + k]
         at_m = index[1, k]
         at_n = index[1, 64 + k]
-        n_re = field[0, at_n]
-        n_im = field[1, at_n]
+        n_re = twice[0, at_n]
+        n_im = twice[1, at_n]
         pair_re = []
         pair_im = []
-        for m in range(MB):
-            m_re = field[0, at_m, m : m + 1, :]
-            m_im = field[1, at_m, m : m + 1, :]
+        for j in range(4):
+            m_re = spread[0, at_m, j]
+            m_im = spread[1, at_m, j]
             pair_re.append(m_re * n_re + m_im * n_im)
             pair_im.append(m_im * n_re - m_re * n_im)
         pairs = jnp.concatenate(
             [jnp.concatenate(pair_re, axis=0), jnp.concatenate(pair_im, axis=0)], axis=1
-        ).astype(BF16)
+        )
         low = coeff_ref[0, k]
         high = coeff_ref[1, k]
         table = jnp.concatenate(
             [low[:, :64], low[:, 64:], high[:, :64], high[:, 64:]], axis=0
         )
         weighted = jnp.dot(table, pairs, preferred_element_type=F32)
-        term_re = jnp.zeros((MB, 256), F32)
-        term_im = jnp.zeros((MB, 256), F32)
-        for l in range(MB):
-            w_re = weighted[8 * l : 8 * l + 8, :256]
-            w_im = weighted[8 * l : 8 * l + 8, 256:]
-            l_re = field[0, at_l, l : l + 1, :]
-            l_im = field[1, at_l, l : l + 1, :]
-            term_re = term_re + (w_re * l_re - w_im * l_im)
-            term_im = term_im + (w_re * l_im + w_im * l_re)
-        total[0, at_p] -= kerr_strength * term_im
-        total[1, at_p] += kerr_strength * term_re
+        weighted = weighted.astype(BF16)
+        term_re = None
+        for j in range(4):
+            w_re = weighted[16 * j : 16 * j + 16, :256]
+            w_im = weighted[16 * j : 16 * j + 16, 256:]
+            l_re = spread[0, at_l, j]
+            l_im = spread[1, at_l, j]
+            one_re = w_re * l_re - w_im * l_im
+            one_im = w_re * l_im + w_im * l_re
+            term_re = one_re if j == 0 else term_re + one_re
+            term_im = one_im if j == 0 else term_im + one_im
+        term_re = term_re.astype(F32)
+        term_im = term_im.astype(F32)
+        total[0, at_p] -= kerr_strength * (term_im[:8] + term_im[8:])
+        total[1, at_p] += kerr_strength * (term_re[:8] + term_re[8:])
 
     for b in range(NMB):
         new = (total[0, b], total[1, b])
@@ -183,7 +196,8 @@
         in_specs=[in_vmem(), in_vmem()],
         out_specs=in_vmem(),
         scratch_shapes=[
-            pltpu.VMEM((2, NMB, MB, 256), F32),
+            pltpu.VMEM((2, NMB, 4, 16, 256), BF16),
+            pltpu.VMEM((2, NMB, 16, 256), BF16),
             pltpu.VMEM((2, NMB, MB, 256), F32),
         ],
         compiler_params=params(),

time: 106 us -> 105 us (level)
  no operation moved by 1% of the time
where the time goes in v5:
time: 105 us; the launch traced here: 104 us
  blocking collectives  97.4 us (93%)
  Pallas kernels  6.65 us (6%)
    all_to_all x4, blocking collectives, swap(): return lax.all_to_all(array, axes, split_axis=0, concat_axis=0, tiled=True)  85.2 us
    all_gather x1, blocking collectives, shards(): return add(own, lax.all_gather(send, 'c', axis=0, tiled=False))  6.53 us
    all_gather x1, blocking collectives, shards(): coeff = lax.all_gather(halves, 'c', axis=0, tiled=False)  5.65 us
    pallas_call x1, Pallas kernels, kerr_step(): pl.pallas_call(kerr_kernel, out_shape=jax.ShapeDtypeStruct((NDEV, 16, 128...  2.43 us

profile of v5, /device:TPU:1, one launch (start us, length us, event | category | flops | bytes accessed | tf_op | source)
XLA Modules:
  0.0 104.3 jit_solution(9029275073313525649)
XLA Ops:
  0.0 2.0 %pack.1 = bf16[64,17,2,128]{3,2,1,0:T(2,128)(2,1)} custom-call(s32[1,4]{1,0:T(1,128)} %list_hbm.1, bf16[2,1,4,16384]{3,2,1,0:T(4,128)(2,1)} %field_hbm.1, bf16[1,64,64]{2,1,0:T(8,128)(2,1)} %coeff_hbm.1), custom_call_target="tpu_custom_call" | custom-call | tf_op jit(solution)/shard_map/pack/pallas_call | solution.py:97
  2.0 34.0 %all_to_all.20.data_ref = bf16[64,17,2,128]{3,2,1,0:T(2,128)(2,1)S(1)} all-to-all(bf16[64,17,2,128]{3,2,1,0:T(2,128)(2,1)} %pack.1), channel_id=1, replica_groups=mesh['y'=8,'z'=8,'x'=4,'c'=2] {'y','z'}, dimensions={0} | all-to-all | bytes 1114112 | tf_op jit(solution)/shard_map/all_to_all | solution.py:366
  36.0 0.2 slice.4
  36.2 5.6 %all_gather.9.coeff_ref = bf16[2,64,16,128]{3,2,1,0:T(8,128)(2,1)S(1)} all-gather(bf16[1,64,16,128]{3,2,1,0:T(8,128)(2,1)S(1)} %bitcast.3), channel_id=1, replica_groups=mesh['y'=8,'z'=8,'x'=4,'c'=2] {'c'}, dimensions={0}, use_global_device_ids=true | all-gather | bytes 786432 | tf_op jit(solution)/shard_map/all_gather | solution.py:372
  41.8 2.4 %kerr.1 = bf16[64,16,128]{2,1,0:T(8,128)(2,1)S(1)} custom-call(bf16[64,17,2,128]{3,2,1,0:T(2,128)(2,1)S(1)} %all_to_all.20.data_ref, bf16[2,64,16,128]{3,2,1,0:T(8,128)(2,1)S(1)} %all_gather.9.coeff_ref), custom_call_target="tpu_custom_call" | custom-call | tf_op jit(solution)/shard_map/kerr/pallas_call | solution.py:193
  44.3 0.0 copy-start
  44.3 0.0 copy-start.1
  44.3 0.0 copy-start.2
  44.3 18.2 %all_to_all.21.data_ref = bf16[64,16,128]{2,1,0:T(8,128)(2,1)S(1)} all-to-all(bf16[64,16,128]{2,1,0:T(8,128)(2,1)S(1)} %kerr.1), channel_id=1, replica_groups=mesh['y'=8,'z'=8,'x'=4,'c'=2] {'y','z'}, dimensions={0} | all-to-all | bytes 524288 | tf_op jit(solution)/shard_map/all_to_all | solution.py:366
  62.5 0.0 copy-done
  62.5 0.0 copy-done.1
  62.5 0.0 copy-done.2
  62.5 0.6 dft.1
  63.1 17.9 %all_to_all.22.data_ref = bf16[64,16,128]{2,1,0:T(8,128)(2,1)S(1)} all-to-all(bf16[64,16,128]{2,1,0:T(8,128)(2,1)S(1)} %dft.1), channel_id=1, replica_groups=mesh['y'=8,'z'=8,'x'=4,'c'=2] {'y','z'}, dimensions={0} | all-to-all | bytes 524288 | tf_op jit(solution)/shard_map/all_to_all | solution.py:366
  81.0 0.1 order.1
  81.1 15.1 %all_to_all.23.data_ref = bf16[4,2,2,256,128]{4,3,2,1,0:T(8,128)(2,1)S(1)} all-to-all(bf16[4,2,2,256,128]{4,3,2,1,0:T(8,128)(2,1)S(1)} %order.1), channel_id=1, replica_groups=mesh['y'=8,'z'=8,'x'=4,'c'=2] {'x'}, dimensions={0} | all-to-all | bytes 2097152 | tf_op jit(solution)/shard_map/all_to_all | solution.py:366
  96.2 0.7 gram.1
  97.0 6.5 %all-gather = bf16[16,2,32,256]{3,2,1,0:T(8,128)(2,1)S(1)} all-gather(bf16[8,2,32,256]{3,2,1,0:T(8,128)(2,1)S(1)} %get-tuple-element.8), channel_id=2, replica_groups=mesh['y'=8,'z'=8,'x'=4,'c'=2] {'c'}, dimensions={0}, use_global_device_ids=true | all-gather | bytes 786432 | tf_op jit(solution)/shard_map/all_gather | solution.py:377
  103.5 0.8 add.1
Async XLA Ops:
  44.3 18.3 %copy-start = (f32[2,128,128]{2,1,0:T(8,128)S(1)}, f32[2,128,128]{2,1,0:T(8,128)}, u32[]{:S(2)}) copy-start(f32[2,128,128]{2,1,0:T(8,128)} %constant.8.clone.twist_ref) | copy-start | bytes 393220
  44.3 18.3 %copy-start.1 = (bf16[256,256]{1,0:T(8,128)(2,1)S(1)}, bf16[256,256]{1,0:T(8,128)(2,1)}, u32[]{:S(2)}) copy-start(bf16[256,256]{1,0:T(8,128)(2,1)} %constant.7.clone.second_ref) | copy-start | bytes 393220
  44.3 18.2 %copy-start.2 = (bf16[256,256]{1,0:T(8,128)(2,1)S(1)}, bf16[256,256]{1,0:T(8,128)(2,1)}, u32[]{:S(2)}) copy-start(bf16[256,256]{1,0:T(8,128)(2,1)} %constant.6.clone.first_ref) | copy-start | bytes 393220

commit v6 on v5

--- a/solution.py
+++ b/solution.py
@@ -12,8 +12,6 @@
 MB = 8
 FT = 128
 FB = 32
-NT = 16384
-PACK_PARTS = 4
 NMB = 32
 NBLK = 64
 MODES = 256
@@ -39,77 +37,57 @@
     return pl.BlockSpec(memory_space=pltpu.HBM)
 
 
-def pack_kernel(list_hbm, field_hbm, coeff_hbm, out_hbm, listed, field, coeff, out, sems, out_sems):
-    coeff_copy = pltpu.make_async_copy(coeff_hbm, coeff, sems.at[0])
-    list_copy = pltpu.make_async_copy(list_hbm, listed, sems.at[1])
-    coeff_copy.start()
-    list_copy.start()
-    field_copies = []
-    for g in range(PACK_PARTS):
-        times = pl.ds(g * (NT // PACK_PARTS), NT // PACK_PARTS)
-        field_copies.append(
-            pltpu.make_async_copy(
-                field_hbm.at[:, :, :, times], field.at[:, :, :, times], sems.at[2 + g]
-            )
-        )
-        field_copies[g].start()
-    core = lax.axis_index("c")
+def pick_kernel(out_ref):
+    row = lax.broadcasted_iota(jnp.int32, (32, 64), 0) + 32 * lax.axis_index("c")
+    col = lax.broadcasted_iota(jnp.int32, (32, 64), 1)
+    out_ref[...] = (col == (row % MB) * MB + row // MB).astype(F32).astype(BF16)
+
+
+def pick():
+    return pl.pallas_call(
+        pick_kernel,
+        out_shape=jax.ShapeDtypeStruct((32, 64), BF16),
+        out_specs=in_vmem(),
+        compiler_params=params(),
+        cost_estimate=pl.CostEstimate(
+            flops=2 * 10**9, bytes_accessed=2**20, transcendentals=0
+        ),
+        name="pick",
+    )()
+
+
+def pack_kernel(pick_ref, list_ref, field_ref, coeff_ref, out_ref):
     place = lax.axis_index(MODE)
-    row = lax.broadcasted_iota(jnp.int32, (32, 64), 0) + 32 * core
-    col = lax.broadcasted_iota(jnp.int32, (32, 64), 1)
-    pick = (col == (row % MB) * MB + row // MB).astype(F32).astype(BF16)
+    own = jnp.dot(pick_ref[...], coeff_ref[0], preferred_element_type=F32)
+    own = jnp.concatenate([own[:16], own[16:]], axis=1).astype(BF16)
     lane = lax.broadcasted_iota(jnp.int32, (2, 128), 1)
     line = lax.broadcasted_iota(jnp.int32, (2, 128), 0)
-    coeff_copy.wait()
-    own = jnp.dot(pick, coeff[0], preferred_element_type=F32)
-    own = jnp.concatenate([own[:16], own[16:]], axis=1).astype(BF16)
-    list_copy.wait()
     index = jnp.zeros((2, 128), jnp.int32)
     for j in range(4):
         here = (lane == place + 64 * (j % 2)) & (line == j // 2)
-        index = jnp.where(here, listed[0, j], index)
+        index = jnp.where(here, list_ref[0:1, j : j + 1], index)
     index = index.astype(F32).astype(BF16)
-    each = NDEV // PACK_PARTS
-    out_copies = []
-    for g in range(PACK_PARTS):
-        field_copies[g].wait()
-        for i in range(g * each, g * each + each):
-            for tt in range(2):
-                for part in range(2):
-                    at = (2 * i + tt) * 128
-                    tile = field[part, 0, :, at : at + 128]
-                    out[i, 4 * tt + 2 * part] = tile[0:2]
-                    out[i, 4 * tt + 2 * part + 1] = tile[2:4]
-            for q in range(8):
-                out[i, 8 + q] = own[2 * q : 2 * q + 2]
-            out[i, 16] = index
-        receivers = pl.ds(g * each, each)
-        out_copies.append(
-            pltpu.make_async_copy(out.at[receivers], out_hbm.at[receivers], out_sems.at[g])
-        )
-        out_copies[g].start()
-    for copy in out_copies:
-        copy.wait()
+    for i in range(NDEV):
+        for tt in range(2):
+            for part in range(2):
+                at = (2 * i + tt) * 128
+                tile = field_ref[part, 0, :, at : at + 128]
+                out_ref[i, 4 * tt + 2 * part] = tile[0:2]
+                out_ref[i, 4 * tt + 2 * part + 1] = tile[2:4]
+        for q in range(8):
+            out_ref[i, 8 + q] = own[2 * q : 2 * q + 2]
+        out_ref[i, 16] = index
 
 
 def pack(block_list, field, coeff):
-    shape = (NDEV, 17, 2, 128)
     return pl.pallas_call(
         pack_kernel,
-        out_shape=jax.ShapeDtypeStruct(shape, BF16),
-        in_specs=[in_hbm(), in_hbm(), in_hbm()],
-        out_specs=in_hbm(),
-        scratch_shapes=[
-            pltpu.SMEM(block_list.shape, jnp.int32),
-            pltpu.VMEM(field.shape, BF16),
-            pltpu.VMEM(coeff.shape, BF16),
-            pltpu.VMEM(shape, BF16),
-            pltpu.SemaphoreType.DMA((2 + PACK_PARTS,)),
-            pltpu.SemaphoreType.DMA((PACK_PARTS,)),
-        ],
-        compiler_params=params(60 * 2**20),
+        out_shape=jax.ShapeDtypeStruct((NDEV, 17, 2, 128), BF16),
+        in_specs=[in_vmem()] * 4,
+        out_specs=in_vmem(),
+        compiler_params=params(),
         name="pack",
-    )(block_list, field, coeff)
+    )(pick(), block_list, field, coeff)
 
 
 def kerr_kernel(data_ref, coeff_ref, out_ref, spread, twice, total):

time: 105 us -> 104 us (level)
  Pallas kernels: 6.65 us -> 5.11 us
    pallas_call x1 -> x2, Pallas kernels: 1.97 us -> 0.43 us  [the longest x1 0.4 us: pack(): pl.pallas_call(pack_kernel, out_shape=jax.ShapeDtypeStruct((NDEV, 17, 2,...]
where the time goes in v6:
time: 104 us
  blocking collectives  97.2 us (93%)
  Pallas kernels  5.11 us (5%)
  local copies, waits for them, and re-layouts  1.14 us (1%)
    all_to_all x4, blocking collectives, swap(): return lax.all_to_all(array, axes, split_axis=0, concat_axis=0, tiled=True)  85 us
    all_gather x1, blocking collectives, shards(): return add(own, lax.all_gather(send, 'c', axis=0, tiled=False))  6.55 us
    all_gather x1, blocking collectives, shards(): coeff = lax.all_gather(halves, 'c', axis=0, tiled=False)  5.65 us
    pallas_call x1, Pallas kernels, kerr_step(): pl.pallas_call(kerr_kernel, out_shape=jax.ShapeDtypeStruct((NDEV, 16, 128...  2.42 us

profile of v6, /device:TPU:1, one launch (start us, length us, event | category | flops | bytes accessed | tf_op | source)
XLA Modules:
  0.0 103.5 jit_solution(7219195771562159117)
XLA Ops:
  0.0 0.0 copy-start.5
  0.0 0.0 copy-start.4
  0.0 0.0 copy-start
  0.0 0.6 copy-done.5
  0.7 0.1 copy-done.4
  0.7 0.2 copy-done
  1.0 0.4 pack.1
  1.4 33.8 %all_to_all.20.data_ref = bf16[64,17,2,128]{3,2,1,0:T(2,128)(2,1)S(1)} all-to-all(bf16[64,17,2,128]{3,2,1,0:T(2,128)(2,1)S(1)} %pack.1), channel_id=1, replica_groups=mesh['y'=8,'z'=8,'x'=4,'c'=2] {'y','z'}, dimensions={0} | all-to-all | bytes 1114112 | tf_op jit(solution)/shard_map/all_to_all | solution.py:344
  35.2 0.2 slice.4
  35.4 5.6 %all_gather.9.coeff_ref = bf16[2,64,16,128]{3,2,1,0:T(8,128)(2,1)S(1)} all-gather(bf16[1,64,16,128]{3,2,1,0:T(8,128)(2,1)S(1)} %bitcast.3), channel_id=1, replica_groups=mesh['y'=8,'z'=8,'x'=4,'c'=2] {'c'}, dimensions={0}, use_global_device_ids=true | all-gather | bytes 786432 | tf_op jit(solution)/shard_map/all_gather | solution.py:350
  41.0 2.4 %kerr.1 = bf16[64,16,128]{2,1,0:T(8,128)(2,1)S(1)} custom-call(bf16[64,17,2,128]{3,2,1,0:T(2,128)(2,1)S(1)} %all_to_all.20.data_ref, bf16[2,64,16,128]{3,2,1,0:T(8,128)(2,1)S(1)} %all_gather.9.coeff_ref), custom_call_target="tpu_custom_call" | custom-call | tf_op jit(solution)/shard_map/kerr/pallas_call | solution.py:171
  43.5 0.0 copy-start.1
  43.5 0.0 copy-start.2
  43.5 0.0 copy-start.3
  43.5 18.2 %all_to_all.21.data_ref = bf16[64,16,128]{2,1,0:T(8,128)(2,1)S(1)} all-to-all(bf16[64,16,128]{2,1,0:T(8,128)(2,1)S(1)} %kerr.1), channel_id=1, replica_groups=mesh['y'=8,'z'=8,'x'=4,'c'=2] {'y','z'}, dimensions={0} | all-to-all | bytes 524288 | tf_op jit(solution)/shard_map/all_to_all | solution.py:344
  61.7 0.0 copy-done.1
  61.7 0.0 copy-done.2
  61.7 0.0 copy-done.3
  61.7 0.6 dft.1
  62.3 17.8 %all_to_all.22.data_ref = bf16[64,16,128]{2,1,0:T(8,128)(2,1)S(1)} all-to-all(bf16[64,16,128]{2,1,0:T(8,128)(2,1)S(1)} %dft.1), channel_id=1, replica_groups=mesh['y'=8,'z'=8,'x'=4,'c'=2] {'y','z'}, dimensions={0} | all-to-all | bytes 524288 | tf_op jit(solution)/shard_map/all_to_all | solution.py:344
  80.2 0.1 order.1
  80.3 15.1 %all_to_all.23.data_ref = bf16[4,2,2,256,128]{4,3,2,1,0:T(8,128)(2,1)S(1)} all-to-all(bf16[4,2,2,256,128]{4,3,2,1,0:T(8,128)(2,1)S(1)} %order.1), channel_id=1, replica_groups=mesh['y'=8,'z'=8,'x'=4,'c'=2] {'x'}, dimensions={0} | all-to-all | bytes 2097152 | tf_op jit(solution)/shard_map/all_to_all | solution.py:344
  95.4 0.7 gram.1
  96.2 6.6 %all-gather = bf16[16,2,32,256]{3,2,1,0:T(8,128)(2,1)S(1)} all-gather(bf16[8,2,32,256]{3,2,1,0:T(8,128)(2,1)S(1)} %get-tuple-element.8), channel_id=2, replica_groups=mesh['y'=8,'z'=8,'x'=4,'c'=2] {'c'}, dimensions={0}, use_global_device_ids=true | all-gather | bytes 786432 | tf_op jit(solution)/shard_map/all_gather | solution.py:355
  102.7 0.8 add.1
  (1 shorter events, 0.0 us)
Async XLA Ops:
  0.0 0.7 copy-start.5
  0.0 0.7 copy-start.4
  0.0 1.0 copy-start
  43.5 18.3 %copy-start.1 = (f32[2,128,128]{2,1,0:T(8,128)S(1)}, f32[2,128,128]{2,1,0:T(8,128)}, u32[]{:S(2)}) copy-start(f32[2,128,128]{2,1,0:T(8,128)} %constant.8.clone.twist_ref) | copy-start | bytes 393220
  43.5 18.3 %copy-start.2 = (bf16[256,256]{1,0:T(8,128)(2,1)S(1)}, bf16[256,256]{1,0:T(8,128)(2,1)}, u32[]{:S(2)}) copy-start(bf16[256,256]{1,0:T(8,128)(2,1)} %constant.7.clone.second_ref) | copy-start | bytes 393220
  43.5 18.3 %copy-start.3 = (bf16[256,256]{1,0:T(8,128)(2,1)S(1)}, bf16[256,256]{1,0:T(8,128)(2,1)}, u32[]{:S(2)}) copy-start(bf16[256,256]{1,0:T(8,128)(2,1)} %constant.6.clone.first_ref) | copy-start | bytes 393220

commit v7 on v6

--- a/solution.py
+++ b/solution.py
@@ -40,7 +40,8 @@
 def pick_kernel(out_ref):
     row = lax.broadcasted_iota(jnp.int32, (32, 64), 0) + 32 * lax.axis_index("c")
     col = lax.broadcasted_iota(jnp.int32, (32, 64), 1)
-    out_ref[...] = (col == (row % MB) * MB + row // MB).astype(F32).astype(BF16)
+    own = (col == (row % MB) * MB + row // MB).astype(F32)
+    out_ref[...] = (kerr_strength * own).astype(BF16)
 
 
 def pick():
@@ -152,8 +153,8 @@
             term_im = one_im if j == 0 else term_im + one_im
         term_re = term_re.astype(F32)
         term_im = term_im.astype(F32)
-        total[0, at_p] -= kerr_strength * (term_im[:8] + term_im[8:])
-        total[1, at_p] += kerr_strength * (term_re[:8] + term_re[8:])
+        total[0, at_p] -= term_im[:8] + term_im[8:]
+        total[1, at_p] += term_re[:8] + term_re[8:]
 
     for b in range(NMB):
         new = (total[0, b], total[1, b])
@@ -276,20 +277,22 @@
     keep = pl.multiple_of(64 * chip + 32 * core, 32)
     give = pl.multiple_of(64 * chip + 32 * (1 - core), 32)
     lane = lax.broadcasted_iota(jnp.int32, (32, 128), 1) // FB
+    ones = [(lane == band).astype(F32) for band in range(4)]
+    minus = [(-one).astype(BF16) for one in ones]
+    ones = [one.astype(BF16) for one in ones]
     for h in range(2):
         lefts = [[] for _ in range(16)]
         rights = []
         for x in range(4):
             rights += [data_ref[x, h, 0], data_ref[x, h, 1]]
             for side, start in enumerate((keep, give)):
-                row_re = data_ref[x, h, 0, pl.ds(start, 32), :].astype(F32)
-                row_im = data_ref[x, h, 1, pl.ds(start, 32), :].astype(F32)
+                row_re = data_ref[x, h, 0, pl.ds(start, 32), :]
+                row_im = data_ref[x, h, 1, pl.ds(start, 32), :]
                 for band in range(4):
-                    b_re = jnp.where(lane == band, row_re, 0.0)
-                    b_im = jnp.where(lane == band, row_im, 0.0)
                     at = 8 * side + 2 * band
-                    lefts[at] += [b_re.astype(BF16), b_im.astype(BF16)]
-                    lefts[at + 1] += [b_im.astype(BF16), (-b_re).astype(BF16)]
+                    b_im = row_im * ones[band]
+                    lefts[at] += [row_re * ones[band], b_im]
+                    lefts[at + 1] += [b_im, row_re * minus[band]]
         left = jnp.concatenate([jnp.concatenate(p, axis=1) for p in lefts], axis=0)
         right = jnp.concatenate(rights, axis=1)
         result = lax.dot_general(

time: 104 us -> 104 us (level)
  no operation moved by 1% of the time
where the time goes in v7:
time: 104 us; the launch traced here: 103 us
  blocking collectives  97.2 us (93%)
  Pallas kernels  5.03 us (5%)
  local copies, waits for them, and re-layouts  1.14 us (1%)
    all_to_all x4, blocking collectives, swap(): return lax.all_to_all(array, axes, split_axis=0, concat_axis=0, tiled=True)  85 us
    all_gather x1, blocking collectives, shards(): return add(own, lax.all_gather(send, 'c', axis=0, tiled=False))  6.53 us
    all_gather x1, blocking collectives, shards(): coeff = lax.all_gather(halves, 'c', axis=0, tiled=False)  5.65 us
    pallas_call x1, Pallas kernels, kerr_step(): pl.pallas_call(kerr_kernel, out_shape=jax.ShapeDtypeStruct((NDEV, 16, 128...  2.35 us

profile of v7, /device:TPU:1, one launch (start us, length us, event | category | flops | bytes accessed | tf_op | source)
XLA Modules:
  0.0 103.5 jit_solution(2972638041564234201)
XLA Ops:
  0.0 0.0 copy-start.5
  0.0 0.0 copy-start.4
  0.0 0.0 copy-start
  0.0 0.6 copy-done.5
  0.7 0.1 copy-done.4
  0.7 0.2 copy-done
  1.0 0.4 pack.1
  1.4 33.8 %all_to_all.20.data_ref = bf16[64,17,2,128]{3,2,1,0:T(2,128)(2,1)S(1)} all-to-all(bf16[64,17,2,128]{3,2,1,0:T(2,128)(2,1)S(1)} %pack.1), channel_id=1, replica_groups=mesh['y'=8,'z'=8,'x'=4,'c'=2] {'y','z'}, dimensions={0} | all-to-all | bytes 1114112 | tf_op jit(solution)/shard_map/all_to_all | solution.py:347
  35.2 0.2 slice.4
  35.4 5.6 %all_gather.9.coeff_ref = bf16[2,64,16,128]{3,2,1,0:T(8,128)(2,1)S(1)} all-gather(bf16[1,64,16,128]{3,2,1,0:T(8,128)(2,1)S(1)} %bitcast.3), channel_id=1, replica_groups=mesh['y'=8,'z'=8,'x'=4,'c'=2] {'c'}, dimensions={0}, use_global_device_ids=true | all-gather | bytes 786432 | tf_op jit(solution)/shard_map/all_gather | solution.py:353
  41.0 2.3 %kerr.1 = bf16[64,16,128]{2,1,0:T(8,128)(2,1)S(1)} custom-call(bf16[64,17,2,128]{3,2,1,0:T(2,128)(2,1)S(1)} %all_to_all.20.data_ref, bf16[2,64,16,128]{3,2,1,0:T(8,128)(2,1)S(1)} %all_gather.9.coeff_ref), custom_call_target="tpu_custom_call" | custom-call | tf_op jit(solution)/shard_map/kerr/pallas_call | solution.py:172
  43.4 0.0 copy-start.1
  43.4 0.0 copy-start.2
  43.4 0.0 copy-start.3
  43.4 18.2 %all_to_all.21.data_ref = bf16[64,16,128]{2,1,0:T(8,128)(2,1)S(1)} all-to-all(bf16[64,16,128]{2,1,0:T(8,128)(2,1)S(1)} %kerr.1), channel_id=1, replica_groups=mesh['y'=8,'z'=8,'x'=4,'c'=2] {'y','z'}, dimensions={0} | all-to-all | bytes 524288 | tf_op jit(solution)/shard_map/all_to_all | solution.py:347
  61.6 0.0 copy-done.1
  61.7 0.0 copy-done.2
  61.7 0.0 copy-done.3
  61.7 0.6 dft.1
  62.2 17.8 %all_to_all.22.data_ref = bf16[64,16,128]{2,1,0:T(8,128)(2,1)S(1)} all-to-all(bf16[64,16,128]{2,1,0:T(8,128)(2,1)S(1)} %dft.1), channel_id=1, replica_groups=mesh['y'=8,'z'=8,'x'=4,'c'=2] {'y','z'}, dimensions={0} | all-to-all | bytes 524288 | tf_op jit(solution)/shard_map/all_to_all | solution.py:347
  80.1 0.1 order.1
  80.2 15.1 %all_to_all.23.data_ref = bf16[4,2,2,256,128]{4,3,2,1,0:T(8,128)(2,1)S(1)} all-to-all(bf16[4,2,2,256,128]{4,3,2,1,0:T(8,128)(2,1)S(1)} %order.1), channel_id=1, replica_groups=mesh['y'=8,'z'=8,'x'=4,'c'=2] {'x'}, dimensions={0} | all-to-all | bytes 2097152 | tf_op jit(solution)/shard_map/all_to_all | solution.py:347
  95.3 0.7 gram.1
  96.1 6.5 %all-gather = bf16[16,2,32,256]{3,2,1,0:T(8,128)(2,1)S(1)} all-gather(bf16[8,2,32,256]{3,2,1,0:T(8,128)(2,1)S(1)} %get-tuple-element.8), channel_id=2, replica_groups=mesh['y'=8,'z'=8,'x'=4,'c'=2] {'c'}, dimensions={0}, use_global_device_ids=true | all-gather | bytes 786432 | tf_op jit(solution)/shard_map/all_gather | solution.py:358
  102.6 0.8 add.1
  (1 shorter events, 0.0 us)
Async XLA Ops:
  0.0 0.7 copy-start.5
  0.0 0.7 copy-start.4
  0.0 1.0 copy-start
  43.4 18.3 %copy-start.1 = (f32[2,128,128]{2,1,0:T(8,128)S(1)}, f32[2,128,128]{2,1,0:T(8,128)}, u32[]{:S(2)}) copy-start(f32[2,128,128]{2,1,0:T(8,128)} %constant.8.clone.twist_ref) | copy-start | bytes 393220
  43.4 18.3 %copy-start.2 = (bf16[256,256]{1,0:T(8,128)(2,1)S(1)}, bf16[256,256]{1,0:T(8,128)(2,1)}, u32[]{:S(2)}) copy-start(bf16[256,256]{1,0:T(8,128)(2,1)} %constant.7.clone.second_ref) | copy-start | bytes 393220
  43.4 18.2 %copy-start.3 = (bf16[256,256]{1,0:T(8,128)(2,1)S(1)}, bf16[256,256]{1,0:T(8,128)(2,1)}, u32[]{:S(2)}) copy-start(bf16[256,256]{1,0:T(8,128)(2,1)} %constant.6.clone.first_ref) | copy-start | bytes 393220

commit v8 on v6

--- a/solution.py
+++ b/solution.py
@@ -40,7 +40,8 @@
 def pick_kernel(out_ref):
     row = lax.broadcasted_iota(jnp.int32, (32, 64), 0) + 32 * lax.axis_index("c")
     col = lax.broadcasted_iota(jnp.int32, (32, 64), 1)
-    out_ref[...] = (col == (row % MB) * MB + row // MB).astype(F32).astype(BF16)
+    own = (col == (row % MB) * MB + row // MB).astype(F32)
+    out_ref[...] = (kerr_strength * own).astype(BF16)
 
 
 def pick():
@@ -152,8 +153,8 @@
             term_im = one_im if j == 0 else term_im + one_im
         term_re = term_re.astype(F32)
         term_im = term_im.astype(F32)
-        total[0, at_p] -= kerr_strength * (term_im[:8] + term_im[8:])
-        total[1, at_p] += kerr_strength * (term_re[:8] + term_re[8:])
+        total[0, at_p] -= term_im[:8] + term_im[8:]
+        total[1, at_p] += term_re[:8] + term_re[8:]
 
     for b in range(NMB):
         new = (total[0, b], total[1, b])

time: 104 us -> 104 us (level)
  no operation moved by 1% of the time
where the time goes in v8:
time: 104 us; the launch traced here: 103 us
  blocking collectives  97.2 us (93%)
  Pallas kernels  5.03 us (5%)
  local copies, waits for them, and re-layouts  1.14 us (1%)
    all_to_all x4, blocking collectives, swap(): return lax.all_to_all(array, axes, split_axis=0, concat_axis=0, tiled=True)  85 us
    all_gather x1, blocking collectives, shards(): return add(own, lax.all_gather(send, 'c', axis=0, tiled=False))  6.55 us
    all_gather x1, blocking collectives, shards(): coeff = lax.all_gather(halves, 'c', axis=0, tiled=False)  5.65 us
    pallas_call x1, Pallas kernels, kerr_step(): pl.pallas_call(kerr_kernel, out_shape=jax.ShapeDtypeStruct((NDEV, 16, 128...  2.35 us

profile of v8, /device:TPU:1, one launch (start us, length us, event | category | flops | bytes accessed | tf_op | source)
XLA Modules:
  0.0 103.5 jit_solution(3377861927683962080)
XLA Ops:
  0.0 0.0 copy-start.5
  0.0 0.0 copy-start.4
  0.0 0.0 copy-start
  0.0 0.6 copy-done.5
  0.7 0.1 copy-done.4
  0.7 0.2 copy-done
  1.0 0.4 pack.1
  1.4 33.8 %all_to_all.20.data_ref = bf16[64,17,2,128]{3,2,1,0:T(2,128)(2,1)S(1)} all-to-all(bf16[64,17,2,128]{3,2,1,0:T(2,128)(2,1)S(1)} %pack.1), channel_id=1, replica_groups=mesh['y'=8,'z'=8,'x'=4,'c'=2] {'y','z'}, dimensions={0} | all-to-all | bytes 1114112 | tf_op jit(solution)/shard_map/all_to_all | solution.py:345
  35.2 0.2 slice.4
  35.4 5.6 %all_gather.9.coeff_ref = bf16[2,64,16,128]{3,2,1,0:T(8,128)(2,1)S(1)} all-gather(bf16[1,64,16,128]{3,2,1,0:T(8,128)(2,1)S(1)} %bitcast.3), channel_id=1, replica_groups=mesh['y'=8,'z'=8,'x'=4,'c'=2] {'c'}, dimensions={0}, use_global_device_ids=true | all-gather | bytes 786432 | tf_op jit(solution)/shard_map/all_gather | solution.py:351
  41.0 2.3 %kerr.1 = bf16[64,16,128]{2,1,0:T(8,128)(2,1)S(1)} custom-call(bf16[64,17,2,128]{3,2,1,0:T(2,128)(2,1)S(1)} %all_to_all.20.data_ref, bf16[2,64,16,128]{3,2,1,0:T(8,128)(2,1)S(1)} %all_gather.9.coeff_ref), custom_call_target="tpu_custom_call" | custom-call | tf_op jit(solution)/shard_map/kerr/pallas_call | solution.py:172
  43.4 0.0 copy-start.1
  43.4 0.0 copy-start.2
  43.4 0.0 copy-start.3
  43.4 18.2 %all_to_all.21.data_ref = bf16[64,16,128]{2,1,0:T(8,128)(2,1)S(1)} all-to-all(bf16[64,16,128]{2,1,0:T(8,128)(2,1)S(1)} %kerr.1), channel_id=1, replica_groups=mesh['y'=8,'z'=8,'x'=4,'c'=2] {'y','z'}, dimensions={0} | all-to-all | bytes 524288 | tf_op jit(solution)/shard_map/all_to_all | solution.py:345
  61.6 0.0 copy-done.1
  61.7 0.0 copy-done.2
  61.7 0.0 copy-done.3
  61.7 0.6 dft.1
  62.2 17.8 %all_to_all.22.data_ref = bf16[64,16,128]{2,1,0:T(8,128)(2,1)S(1)} all-to-all(bf16[64,16,128]{2,1,0:T(8,128)(2,1)S(1)} %dft.1), channel_id=1, replica_groups=mesh['y'=8,'z'=8,'x'=4,'c'=2] {'y','z'}, dimensions={0} | all-to-all | bytes 524288 | tf_op jit(solution)/shard_map/all_to_all | solution.py:345
  80.1 0.1 order.1
  80.2 15.1 %all_to_all.23.data_ref = bf16[4,2,2,256,128]{4,3,2,1,0:T(8,128)(2,1)S(1)} all-to-all(bf16[4,2,2,256,128]{4,3,2,1,0:T(8,128)(2,1)S(1)} %order.1), channel_id=1, replica_groups=mesh['y'=8,'z'=8,'x'=4,'c'=2] {'x'}, dimensions={0} | all-to-all | bytes 2097152 | tf_op jit(solution)/shard_map/all_to_all | solution.py:345
  95.3 0.7 gram.1
  96.1 6.5 %all-gather = bf16[16,2,32,256]{3,2,1,0:T(8,128)(2,1)S(1)} all-gather(bf16[8,2,32,256]{3,2,1,0:T(8,128)(2,1)S(1)} %get-tuple-element.8), channel_id=2, replica_groups=mesh['y'=8,'z'=8,'x'=4,'c'=2] {'c'}, dimensions={0}, use_global_device_ids=true | all-gather | bytes 786432 | tf_op jit(solution)/shard_map/all_gather | solution.py:356
  102.6 0.8 add.1
  (1 shorter events, 0.0 us)
Async XLA Ops:
  0.0 0.7 copy-start.5
  0.0 0.7 copy-start.4
  0.0 1.0 copy-start
  43.4 18.3 %copy-start.1 = (f32[2,128,128]{2,1,0:T(8,128)S(1)}, f32[2,128,128]{2,1,0:T(8,128)}, u32[]{:S(2)}) copy-start(f32[2,128,128]{2,1,0:T(8,128)} %constant.8.clone.twist_ref) | copy-start | bytes 393220
  43.4 18.3 %copy-start.2 = (bf16[256,256]{1,0:T(8,128)(2,1)S(1)}, bf16[256,256]{1,0:T(8,128)(2,1)}, u32[]{:S(2)}) copy-start(bf16[256,256]{1,0:T(8,128)(2,1)} %constant.7.clone.second_ref) | copy-start | bytes 393220
  43.4 18.3 %copy-start.3 = (bf16[256,256]{1,0:T(8,128)(2,1)S(1)}, bf16[256,256]{1,0:T(8,128)(2,1)}, u32[]{:S(2)}) copy-start(bf16[256,256]{1,0:T(8,128)(2,1)} %constant.6.clone.first_ref) | copy-start | bytes 393220
